TPU v7x, 256 devices: a whole 4x4x8 slice. The times are simulated.
256 devices in a mesh: group: 16 (over x_hi, y, core), roll: 2 (over x_lo), tp: 8 (over z).
Axes of the slice: x: 4 (x_hi: 2, x_lo: 2; x = x_hi * 2 + x_lo), y: 4, z: 8, core: 2. Of those that a mesh axis runs over, the one named last changes fastest.
Arguments:
- vis_hidden: bfloat16 [4096, 5120], P('group'), may hold values from -6 to 6
- merge_weight: bfloat16 [5120, 8192], P('group', ('roll', 'tp')), may hold values from -0.078125 to 0.078125
- merge_bias: float32 [8192], P(('roll', 'tp')), may hold values from -3 to 3
- norm_gain: float32 [8192], replicated, may hold values from 0.1 to 1.9
- kv_weight: bfloat16 [8192, 2048], P(None, 'tp'), may hold values from -0.0625 to 0.0625
- kv_bias: float32 [2048], P('tp'), may hold values from -3 to 3
- queries: bfloat16 [32768, 8192], P(('group', 'roll'), 'tp'), may hold values from -26 to 26
- text_kv: bfloat16 [32768, 2048], P(('group', 'roll'), 'tp'), may hold values from -6 to 6
- image_count: int32 [16], P('group'), may hold values from 64 to 256, as said below
- image_pos: int32 [3, 4096], P(None, 'group'), may hold values from 0 to 4095
- resp_length: int32 [256], P(('group', 'roll')), may hold values from 32 to 128, as said below
Outputs:
- attended: bfloat16 [32768, 8192], P(('group', 'roll'), 'tp')
Inputs may be any that keep to these rules, and one draw needn't show every extreme that they name: `image_count`: each prompt has at least a quarter of its 256 slots live, and some prompt has all 256 live. `resp_length`: each rollout has at least 32 tokens, and some rollout has all 128.
All inputs are finite; a program needn't handle non-finite values.
Results may differ from a plain program's by a relative error of at most 0.005.
Values may be sent and summed in bfloat16 or wider, within the bound.
A program may use at most 64 MiB of HBM per device.

v0:
```python
import jax
import jax.numpy as jnp
from jax import lax
from jax.sharding import PartitionSpec as P

HEAD_DIM = 128
RLEN = 128


def rotate(key_part, positions):
    half_dim = key_part.shape[-1] // 2
    inverse = 1000000.0 ** (-jnp.arange(half_dim, dtype=jnp.float32) * 2.0 / key_part.shape[-1])
    freq_index = jnp.arange(half_dim)
    first_cut = half_dim // 4
    second_cut = first_cut + 3 * half_dim // 8
    pos_f = positions.astype(jnp.float32)
    chosen = jnp.where(
        freq_index[None, :] < first_cut,
        pos_f[0][:, None],
        jnp.where(freq_index[None, :] < second_cut, pos_f[1][:, None], pos_f[2][:, None]),
    )
    angles = (chosen * inverse)[:, None, :]
    cosine = jnp.cos(angles)
    sine_part = jnp.sin(angles)
    first_half = key_part[..., :half_dim]
    second_half = key_part[..., half_dim:]
    return jnp.concatenate(
        [
            first_half * cosine - second_half * sine_part,
            second_half * cosine + first_half * sine_part,
        ],
        axis=-1,
    )


def project(full_rows, positions, norm_gain, kv_weight, kv_bias):
    values_f = full_rows.astype(jnp.float32)
    inv_rms = lax.rsqrt(jnp.mean(values_f * values_f, axis=-1, keepdims=True) + 1e-06)
    normed = (values_f * inv_rms * norm_gain).astype(jnp.bfloat16)
    projected = jnp.dot(normed, kv_weight, preferred_element_type=jnp.float32) + kv_bias
    projected = projected.reshape(full_rows.shape[0], -1, 2, HEAD_DIM)
    image_keys = rotate(projected[:, :, 0], positions).astype(jnp.bfloat16)
    image_values = projected[:, :, 1].astype(jnp.bfloat16)
    return (image_keys, image_values)


def body(
    vis_hidden,
    merge_weight,
    merge_bias,
    norm_gain,
    kv_weight,
    kv_bias,
    queries,
    text_kv,
    image_count,
    image_pos,
    resp_length,
):
    activated = jax.nn.gelu(vis_hidden.astype(jnp.float32), approximate=False).astype(jnp.bfloat16)
    merged = jnp.dot(
        activated,
        lax.all_gather(merge_weight, "group", axis=0, tiled=True),
        preferred_element_type=jnp.float32,
    )
    visual = (merged + merge_bias).astype(jnp.bfloat16)
    full_rows = lax.all_gather(visual, ("roll", "tp"), axis=1, tiled=True)
    image_keys, image_values = project(full_rows, image_pos, norm_gain, kv_weight, kv_bias)
    rollouts = resp_length.shape[0]
    kv_local = text_kv.shape[1] // (2 * HEAD_DIM)
    per_group = queries.shape[1] // (HEAD_DIM * kv_local)
    shaped_q = queries.reshape(rollouts, RLEN, kv_local, per_group, HEAD_DIM)
    shaped_kv = text_kv.reshape(rollouts, RLEN, kv_local, 2, HEAD_DIM)
    factor = HEAD_DIM ** (-0.5)
    image_scores = (
        jnp.einsum("rtkgd,jkd->rkgtj", shaped_q, image_keys, preferred_element_type=jnp.float32)
        * factor
    )
    text_scores = (
        jnp.einsum(
            "rtkgd,rjkd->rkgtj", shaped_q, shaped_kv[:, :, :, 0], preferred_element_type=jnp.float32
        )
        * factor
    )
    image_live = jnp.arange(image_keys.shape[0]) < image_count[0]
    causal = jnp.arange(RLEN)[:, None] >= jnp.arange(RLEN)[None, :]
    image_scores = jnp.where(image_live, image_scores, -1e30)
    text_scores = jnp.where(causal, text_scores, -1e30)
    highest = jnp.maximum(jnp.max(image_scores, axis=-1), jnp.max(text_scores, axis=-1))[..., None]
    image_exp = jnp.exp(image_scores - highest)
    text_exp = jnp.exp(text_scores - highest)
    denominator = jnp.sum(image_exp, axis=-1, keepdims=True) + jnp.sum(
        text_exp, axis=-1, keepdims=True
    )
    image_weights = (image_exp / denominator).astype(jnp.bfloat16)
    text_weights = (text_exp / denominator).astype(jnp.bfloat16)
    context = jnp.einsum(
        "rkgtj,jkd->rtkgd", image_weights, image_values, preferred_element_type=jnp.float32
    )
    context = context + jnp.einsum(
        "rkgtj,rjkd->rtkgd", text_weights, shaped_kv[:, :, :, 1], preferred_element_type=jnp.float32
    )
    live_rows = jnp.arange(RLEN)[None, :] < resp_length[:, None]
    context = jnp.where(live_rows[:, :, None, None, None], context, 0.0)
    return context.reshape(queries.shape).astype(jnp.bfloat16)


def solution(mesh):
    in_specs = (
        P("group", None),
        P("group", ("roll", "tp")),
        P(("roll", "tp")),
        P(),
        P(None, "tp"),
        P("tp"),
        P(("group", "roll"), "tp"),
        P(("group", "roll"), "tp"),
        P("group"),
        P(None, "group"),
        P(("group", "roll")),
    )
    out_specs = P(("group", "roll"), "tp")
    return jax.shard_map(body, mesh=mesh, in_specs=in_specs, out_specs=out_specs, check_vma=False)
```

profile of v0, /device:TPU:6, one launch (start us, length us, event | category | flops | bytes accessed | tf_op | source)
XLA Modules:
  0.0 198.6 jit_solution(13274173615900657364)
XLA Ops:
  6.5 0.0 all-gather.3.cloned.1.call-start
  6.5 0.7 all-gather.3.cloned.1.call-update
  7.3 0.0 copy-start.2
  7.3 0.0 copy-start.1
  7.3 0.0 all-gather.5.cloned.1.call-start
  7.3 69.0 %all-gather.3.cloned.1.call-done = bf16[5120,512]{1,0:T(8,128)(2,1)} async-done(((bf16[320,512]{1,0:T(8,128)(2,1)}), bf16[5120,512]{1,0:T(8,128)(2,1)}) %all-gather.3.cloned.1.call-update) | async-done | bytes 5242896 | tf_op jit(solution)/shard_map/all_gather | solution.py:63
  76.3 14.1 %fusion.61 = bf16[256,512]{1,0:T(8,128)(2,1)} fusion(bf16[5120,512]{1,0:T(8,128)(2,1)} %all-gather.3.cloned.1.call-done, bf16[256,5120]{1,0:T(8,128)(2,1)} %param.11, f32[512]{0:T(512)} %param.13), kind=kOutput, calls=%fused_computation.71 | convolution fusion | flops 1428946944 | bytes 8128512 | tf_op jit(solution)/shard_map/dot_general | solution.py:61
  90.4 0.0 copy-start.5
  90.4 0.0 all-gather.5.cloned.1.call-update
  90.4 0.0 copy-done.2
  91.1 2.2 %copy.41 = bf16[128,8,8,128]{3,2,1,0:T(8,128)(2,1)S(1)} copy(bf16[128,8,8,128]{3,1,2,0:T(8,128)(2,1)} %bitcast.113) | data formatting | bytes 4194304
  93.3 0.0 copy-done.1
  93.3 0.1 reshape.446
  93.5 0.0 copy-done.5
  93.5 0.1 iota_compare_fusion.1
  93.6 0.7 fusion.110
  94.4 0.0 copy-start.3
  94.4 0.0 copy-start.4
  94.4 2.9 %fusion.46 = (f32[8,8,128]{2,1,0:T(8,128)S(1)}, f32[8,128,128,8]{2,1,3,0:T(8,128)}) fusion(pred[128,128]{0,1:T(8,128)(4,1)S(1)} %iota_compare_fusion, bf16[8,128,8,128]{3,2,1,0:T(8,128)(2,1)S(1)} %bitcast.110, bf16[8,128,1,1,128]{4,3,1,0,2:T(2,128)(2,1)S(1)} %get-tuple-element.6), kind=kOutput, calls=%fused_computation.58 | convolution fusion | flops 271572992 | bytes 6602752 | tf_op jit(solution)/shard_map/rtkgd,rjkd->rkgtj/dot_general | solution.py:80
  97.3 69.0 %all-gather.5.cloned.1.call-done = bf16[256,8192]{1,0:T(8,128)(2,1)} async-done(((bf16[256,512]{1,0:T(8,128)(2,1)}), bf16[256,8192]{1,0:T(8,128)(2,1)}) %all-gather.5.cloned.1.call-update) | async-done | bytes 4194320 | tf_op jit(solution)/shard_map/all_gather | solution.py:67
  166.3 3.1 %fusion = f32[256]{0:T(256)S(1)} fusion(bf16[256,8192]{1,0:T(8,128)(2,1)} %all-gather.5.cloned.1.call-done), kind=kLoop, calls=%fused_computation.2 | loop fusion | flops 6291200 | bytes 4195328 | tf_op jit(solution)/shard_map/reduce_sum | solution.py:38
  169.4 0.0 copy-done.3
  169.4 0.0 copy-done.4
  169.4 5.6 %fusion.64 = f32[256,256]{0,1:T(8,128)S(1)} fusion(bf16[8192,256]{1,0:T(8,128)(2,1)} %param.15, bf16[256,8192]{1,0:T(8,128)(2,1)} %all-gather.5.cloned.1.call-done, f32[8192]{0:T(1024)S(1)} %copy-done.3, f32[256]{0:T(256)S(1)} %add_rsqrt_fusion, f32[256]{0:T(256)S(1)} %copy-done.4), kind=kOutput, calls=%fused_computation.72 | convolution fusion | flops 1082195968 | bytes 8685568 | tf_op jit(solution)/shard_map/dot_general | solution.py:40
  175.0 0.1 copy.38
  175.1 0.6 fusion.73
  175.7 1.6 bitcast_reduce_fusion
  177.3 0.0 copy-start
  177.3 2.6 %fusion.4 = f32[8,8,128]{2,1,0:T(8,128)S(1)} fusion(f32[256,8,128,8]{2,0,3,1:T(8,128)S(1)} %get-tuple-element.13, f32[8,8,128]{2,1,0:T(8,128)S(1)} %max.9, pred[256]{0:T(512)(128)(4,1)S(1)} %iota_compare_fusion.2), kind=kLoop, calls=%fused_computation.13 | loop fusion | flops 8380416 | bytes 8454400 | tf_op jit(solution)/shard_map/reduce_sum | solution.py:92
  179.8 0.0 copy-done
  179.9 1.2 fusion.45
  181.1 2.4 %fusion.40 = f32[128,8,8,128]{3,0,2,1:T(8,128)S(1)} fusion(f32[256,8,128,8]{2,0,3,1:T(8,128)S(1)} %get-tuple-element.13, f32[8,8,128]{2,1,0:T(8,128)S(1)} %add.48, f32[8,8,128]{2,1,0:T(8,128)S(1)} %max.9, pred[256]{0:T(512)(128)(4,1)S(1)} %iota_compare_fusion.2, f32[256,1,2,128]{0,3,2,1:T(8,128)S(1)} %bitcast.116), kind=kOutput, calls=%fused_computation.50 | convolution fusion | flops 547356672 | bytes 12714496 | tf_op jit(solution)/shard_map/rkgtj,jkd->rtkgd/dot_general | solution.py:97
  183.5 3.1 %fusion.39 = bf16[8,128,1,8,128]{1,4,3,0,2:T(8,128)(2,1)} fusion(f32[128,8,8,128]{3,0,2,1:T(8,128)S(1)} %fusion.40, f32[8,128,128,8]{2,1,3,0:T(8,128)S(1)} %copy-done, f32[8,8,128]{2,1,0:T(8,128)S(1)} %add.48, f32[8,8,128]{2,1,0:T(8,128)S(1)} %max.9, pred[128,128]{0,1:T(8,128)(4,1)S(1)} %iota_compare_fusion, pred[8,128]{1,0:T(8,128)(4,1)S(1)} %iota_compare_fusion.1, ...), kind=kOutput, calls=%fused_computation.48 | convolution fusion | flops 276824064 | bytes 10830848 | tf_op jit(solution)/shard_map/rkgtj,rjkd->rtkgd/dot_general | solution.py:100
  186.6 3.2 %copy.27 = bf16[8,128,1,8,128]{4,3,1,0,2:T(8,128)(2,1)S(1)} copy(bf16[8,128,1,8,128]{1,4,3,0,2:T(8,128)(2,1)} %fusion.39) | data formatting | bytes 4194304 | tf_op jit(solution)/shard_map/convert_element_type | solution.py:105
  189.8 1.9 copy.58
  (10 shorter events, 0.1 us)
Async XLA Ops:
  6.5 69.8 %all-gather.3.cloned.1.call-start = ((), (), s32[]{:S(2)}) async-start(), calls=%async_computation | async-start | bytes 5570560 | tf_op jit(solution)/shard_map/all_gather | solution.py:63
  7.3 83.2 %copy-start.2 = (s32[3,256]{1,0:T(4,128)S(1)}, s32[3,256]{1,0:T(4,128)}, u32[]{:S(2)}) copy-start(s32[3,256]{1,0:T(4,128)} %param.20) | copy-start | bytes 9220
  7.3 86.1 %copy-start.1 = (bf16[1024,256]{1,0:T(8,128)(2,1)S(1)}, bf16[1024,256]{1,0:T(8,128)(2,1)}, u32[]{:S(2)}) copy-start(bf16[1024,256]{1,0:T(8,128)(2,1)} %param.18) | copy-start | bytes 1572868
  7.3 159.0 %all-gather.5.cloned.1.call-start = ((), (), s32[]{:S(2)}) async-start(), calls=%async_computation.1 | async-start | bytes 4456448 | tf_op jit(solution)/shard_map/all_gather | solution.py:67
  90.4 3.1 %copy-start.5 = (s32[8]{0:T(128)S(1)}, s32[8]{0:T(128)}, u32[]{:S(2)}) copy-start(s32[8]{0:T(128)} %param.21) | copy-start | bytes 100
  94.4 75.0 %copy-start.3 = (f32[8192]{0:T(1024)S(1)}, f32[8192]{0:T(1024)}, u32[]{:S(2)}) copy-start(f32[8192]{0:T(1024)} %param.14) | copy-start | bytes 98308
  94.4 75.0 %copy-start.4 = (f32[256]{0:T(256)S(1)}, f32[256]{0:T(256)}, u32[]{:S(2)}) copy-start(f32[256]{0:T(256)} %param.16) | copy-start | bytes 3076
  177.3 2.6 %copy-start = (f32[8,128,128,8]{2,1,3,0:T(8,128)S(1)}, f32[8,128,128,8]{2,1,3,0:T(8,128)}, u32[]{:S(2)}) copy-start(f32[8,128,128,8]{2,1,3,0:T(8,128)} %get-tuple-element.15) | copy-start | bytes 12582916
Sparse Core Ops, SparseCore 0:
  10.1 66.1 all-gather.2
  90.6 75.6 all-gather.4
where the time goes:
time: 199 us
  waiting for transfers between devices  139 us (70%)
  matrix products  29.6 us (15%)
  between operations  14.3 us (7%)
  local copies, waits for them, and re-layouts  8.35 us (4%)
  other arithmetic  7.61 us (4%)
    all_gather x1, waiting for transfers between devices, body(): lax.all_gather(merge_weight, 'group', axis=0, tiled=True)  69 us
    all_gather x1, waiting for transfers between devices, body(): full_rows = lax.all_gather(visual, ('roll', 'tp'), axis=1, tiled=True)  69 us
    dot_general x1, matrix products, body(): jnp.dot(activated, lax.all_gather(merge_weight, 'group', axis=0, tiled=Tr...  14.1 us
    dot_general x1, matrix products, project(): jnp.dot(normed, kv_weight, preferred_element_type=jnp.float32) + kv_bias  5.56 us
    unnamed x15, local copies, waits for them, and re-layouts  4.27 us
  transfers between devices with their start and end apart: 2, of which 2 were waited for; matrix products, arithmetic and copies ran while one was open for 3% of the time, Pallas kernels for 0%

commit v1 on v0

v1 whole, which is shorter than its diff:
```python
import math

import jax
import jax.numpy as jnp
from jax import lax
from jax.experimental import pallas as pl
from jax.experimental.pallas import tpu as pltpu
from jax.sharding import PartitionSpec as P

HEAD_DIM = 128
RLEN = 128
MESH = pl.DeviceIdType.MESH
BF16 = jnp.bfloat16
F32 = jnp.float32

ZOFF = (0, 1, -1, 2, -2, 3, -3, 4)
ZBACK = (0, 2, 1, 4, 3, 6, 5, 7)
KVGROUPS = ((0, 3), (3, 2), (5, 3))
ROWS = 256
HALF = 128
HID = 320
PAIR = 640
COLS = 512


def gather_project_kernel(
    vis_hbm,
    w_hbm,
    kvw_hbm,
    mbias_ref,
    gain_ref,
    kvbias_ref,
    cos_ref,
    sin_ref,
    out_ref,
    vis,
    act,
    wbuf,
    kvbuf,
    acc,
    visual,
    xs,
    xg,
    sumsq,
    sumsq_in,
    sbuf,
    rbuf,
    res,
    res_in,
    local_sem,
    w_send,
    w_recv,
    kz_send,
    kz_recv,
    kx_send,
    kx_recv,
    v_sem,
    q_send,
    q_recv,
    p_send,
    p_recv,
    o_sem,
):
    g = lax.axis_index("group")
    roll = lax.axis_index("roll")
    z = lax.axis_index("tp")
    hi = g // 8
    y = lax.rem(g // 2, 4)
    core = lax.rem(g, 2)
    x = 2 * hi + roll
    me_k = hi * 4 + y

    def at(dx=0, dy=0, dz=0, sib=False):
        xx = lax.rem(x + dx + 4, 4)
        yy = lax.rem(y + dy + 4, 4)
        zz = lax.rem(z + dz + 8, 8)
        cc = 1 - core if sib else core
        return ((xx // 2) * 8 + yy * 2 + cc, lax.rem(xx, 2), zz)

    def k_of(dh, dy):
        hh = 1 - hi if dh else hi
        return hh * 4 + lax.rem(y + dy + 4, 4)

    started = []

    def send(src, dst, ssem, rsem, device):
        copy = pltpu.make_async_remote_copy(
            src_ref=src,
            dst_ref=dst,
            send_sem=ssem,
            recv_sem=rsem,
            device_id=device,
            device_id_type=MESH,
        )
        copy.start()
        started.append(copy)

    def arrived(dst, rsem):
        pltpu.make_async_remote_copy(
            src_ref=dst,
            dst_ref=dst,
            send_sem=rsem,
            recv_sem=rsem,
            device_id=at(sib=True),
            device_id_type=MESH,
        ).wait_recv()

    quarter = x * 2 + core
    kv_part = pl.ds(pl.multiple_of(quarter * HALF, HALF), HALF)

    def kv_rows(zz):
        start = (quarter // 4) * 4096 + zz * COLS + lax.rem(quarter, 4) * HALF
        return pl.ds(pl.multiple_of(start, HALF), HALF)

    own_w = pltpu.make_async_copy(
        w_hbm, wbuf.at[me_k, pl.ds(pl.multiple_of(core * HID, HID), HID)], local_sem.at[0]
    )
    own_kv = pltpu.make_async_copy(kvw_hbm.at[kv_rows(z)], kvbuf.at[0, kv_part], local_sem.at[1])
    own_vis = pltpu.make_async_copy(vis_hbm, vis, local_sem.at[2])
    own_w.start()
    own_kv.start()
    own_vis.start()

    partners = [at(dx=1), at(dx=-1), at(dx=2), at(dy=1), at(dy=-1), at(dy=2), at(sib=True)]
    partners += [at(dz=d) for d in ZOFF[1:]]
    barrier = pltpu.get_barrier_semaphore()
    for partner in partners:
        pl.semaphore_signal(barrier, inc=1, device_id=partner, device_id_type=MESH)
    pl.semaphore_wait(barrier, len(partners))

    def w_half(k, cc):
        return wbuf.at[k, pl.ds(pl.multiple_of(cc * HID, HID), HID)]

    slots = [(0, 0), (0, 1), (0, -1), (1, 0), (0, 2), (1, 1), (1, -1), (1, 2)]
    sent = iter(range(64))

    def w_forward(slot, targets):
        dh, dy = slots[slot]
        block = w_half(k_of(dh, dy), core)
        for dx, ddy in targets:
            there = ((dh + (1 if dx else 0)) % 2, (dy - ddy) % 4)
            index = [(a, b % 4) for a, b in slots].index(there)
            send(block, block, w_send.at[next(sent)], w_recv.at[index], at(dx=dx, dy=ddy))

    def w_sibling(slot):
        dh, dy = slots[slot]
        block = w_half(k_of(dh, dy), core)
        send(block, block, w_send.at[next(sent)], w_recv.at[8 + slot], at(sib=True))

    def w_wait(slot, from_sibling=False):
        dh, dy = slots[slot]
        cc = 1 - core if from_sibling else core
        arrived(w_half(k_of(dh, dy), cc), w_recv.at[8 * from_sibling + slot])

    own_w.wait()
    w_forward(0, [(2, 0)])
    for j in (7, 5, 6, 3, 4, 1, 2):
        zz = lax.rem(z + ZOFF[j] + 8, 8)
        send(
            kvw_hbm.at[kv_rows(zz)],
            kvbuf.at[ZBACK[j], kv_part],
            kz_send.at[j],
            kz_recv.at[ZBACK[j]],
            at(dz=ZOFF[j]),
        )
    w_forward(0, [(0, 1), (0, -1), (0, 2)])
    w_sibling(0)

    own_vis.wait()
    for k in range(8):
        v = vis[:, k * PAIR : (k + 1) * PAIR].astype(F32)
        act[k] = (v * (1.0 + lax.erf(v * (1.0 / math.sqrt(2.0)))) * 0.5).astype(BF16)

    def merge(slot, first=False):
        k = k_of(*slots[slot])
        part = jnp.dot(act[k], wbuf[k], preferred_element_type=F32)
        if first:
            acc[...] = part
        else:
            acc[...] += part

    kx_sent = iter(range(64))

    def kv_block(group, part):
        first, count = KVGROUPS[group]
        return kvbuf.at[pl.ds(first, count), pl.ds(pl.multiple_of(part * HALF, HALF), HALF)]

    def kv_share(group):
        first, count = KVGROUPS[group]
        for j in range(first, first + count):
            if j:
                arrived(kvbuf.at[j, kv_part], kz_recv.at[j])
        block = kv_block(group, quarter)
        for dx, source in ((2, 3), (1, 2), (-1, 1)):
            send(block, block, kx_send.at[next(kx_sent)], kx_recv.at[group * 7 + source], at(dx=dx))
        send(block, block, kx_send.at[next(kx_sent)], kx_recv.at[group * 7], at(sib=True))

    def part_at(dx, cc):
        return lax.rem(x + dx + 4, 4) * 2 + cc

    def kv_pass(group):
        for dx, source in ((1, 1), (-1, 2), (2, 3)):
            block = kv_block(group, part_at(dx, core))
            arrived(block, kx_recv.at[group * 7 + source])
            send(
                block,
                block,
                kx_send.at[next(kx_sent)],
                kx_recv.at[group * 7 + 3 + source],
                at(sib=True),
            )

    def kv_end(group):
        arrived(kv_block(group, part_at(0, 1 - core)), kx_recv.at[group * 7])
        for dx, source in ((1, 4), (-1, 5), (2, 6)):
            arrived(kv_block(group, part_at(dx, 1 - core)), kx_recv.at[group * 7 + source])

    own_kv.wait()
    w_wait(3)
    w_forward(3, [(0, 1), (0, -1), (0, 2)])
    w_sibling(3)
    kv_share(0)
    w_wait(0, True)
    merge(0, True)
    for slot in (1, 2):
        w_wait(slot)
        w_sibling(slot)
    kv_share(1)
    w_wait(3, True)
    merge(3)
    w_wait(4)
    w_sibling(4)
    kv_share(2)
    for slot in (1, 2, 4):
        w_wait(slot, True)
        merge(slot)
    kv_pass(0)
    for slot in (5, 6):
        w_wait(slot)
        w_sibling(slot)
    kv_pass(1)
    w_wait(7)
    w_sibling(7)
    kv_pass(2)
    for slot in (5, 6, 7):
        w_wait(slot, True)
        merge(slot)

    visual[...] = (acc[...] + mbias_ref[...]).astype(BF16)
    mine = pl.ds(pl.multiple_of(roll * HALF, HALF), HALF)
    theirs = pl.ds(pl.multiple_of((1 - roll) * HALF, HALF), HALF)
    partner = (g, 1 - roll, z)
    send(visual.at[theirs], xs.at[roll], v_sem.at[0], v_sem.at[1], partner)
    xs[roll] = visual[mine, :]
    for group in range(3):
        kv_end(group)
    arrived(xs.at[1 - roll], v_sem.at[1])

    total = jnp.zeros((HALF, 1), F32)
    for r in range(2):
        start = pl.multiple_of(r * 4096 + z * COLS, COLS)
        v = xs[r].astype(F32)
        total += jnp.sum(v * v, axis=1, keepdims=True)
        xg[r] = (v * gain_ref[:, pl.ds(start, COLS)]).astype(BF16)
    sumsq[...] = jnp.broadcast_to(total, (HALF, HALF)).T[:8]
    for j in range(1, 8):
        send(sumsq, sumsq_in.at[ZBACK[j]], q_send.at[j], q_recv.at[ZBACK[j]], at(dz=ZOFF[j]))

    def product(j):
        return jnp.dot(xg[0], kvbuf[j, :COLS], preferred_element_type=F32) + jnp.dot(
            xg[1], kvbuf[j, COLS:], preferred_element_type=F32
        )

    for j in (7, 5, 6, 3, 4, 1, 2):
        sbuf[j] = product(j).astype(BF16)
        send(sbuf.at[j], rbuf.at[ZBACK[j]], p_send.at[j], p_recv.at[ZBACK[j]], at(dz=ZOFF[j]))
    proj = product(0)
    square = sumsq[...]
    for j in range(1, 8):
        arrived(sumsq_in.at[j], q_recv.at[j])
        square += sumsq_in[j]
    inv = lax.rsqrt(square * (1.0 / 8192.0) + 1e-06)
    inv = jnp.broadcast_to(inv[:1], (HALF, HALF)).T
    for j in (1, 2, 3, 4, 5, 6, 7):
        arrived(rbuf.at[j], p_recv.at[j])
        proj += rbuf[j].astype(F32)
    key = proj[:, :HEAD_DIM] * inv + kvbias_ref[:, :HEAD_DIM]
    value = proj[:, HEAD_DIM:] * inv + kvbias_ref[:, HEAD_DIM:]
    key = key * cos_ref[mine, :] + pltpu.roll(key, HEAD_DIM // 2, 1) * sin_ref[mine, :]
    res[:, :HEAD_DIM] = key.astype(BF16)
    res[:, HEAD_DIM:] = value.astype(BF16)
    send(res, res_in, o_sem.at[0], o_sem.at[1], partner)
    out_ref[mine, :] = res[...]
    arrived(res_in, o_sem.at[1])
    out_ref[theirs, :] = res_in[...]
    for copy in started:
        copy.wait_send()


def gather_project(vis, w, kvw, mbias, gain, kvbias, cos, sin):
    vmem = pl.BlockSpec(memory_space=pltpu.VMEM)
    hbm = pl.BlockSpec(memory_space=pl.ANY)
    dma = pltpu.SemaphoreType.DMA
    return pl.pallas_call(
        gather_project_kernel,
        out_shape=jax.ShapeDtypeStruct((ROWS, 2 * HEAD_DIM), BF16),
        in_specs=[hbm, hbm, hbm, vmem, vmem, vmem, vmem, vmem],
        out_specs=vmem,
        scratch_shapes=[
            pltpu.VMEM((ROWS, 5120), BF16),
            pltpu.VMEM((8, ROWS, PAIR), BF16),
            pltpu.VMEM((8, PAIR, COLS), BF16),
            pltpu.VMEM((8, 1024, 2 * HEAD_DIM), BF16),
            pltpu.VMEM((ROWS, COLS), F32),
            pltpu.VMEM((ROWS, COLS), BF16),
            pltpu.VMEM((2, HALF, COLS), BF16),
            pltpu.VMEM((2, HALF, COLS), BF16),
            pltpu.VMEM((8, HALF), F32),
            pltpu.VMEM((8, 8, HALF), F32),
            pltpu.VMEM((8, HALF, 2 * HEAD_DIM), BF16),
            pltpu.VMEM((8, HALF, 2 * HEAD_DIM), BF16),
            pltpu.VMEM((HALF, 2 * HEAD_DIM), BF16),
            pltpu.VMEM((HALF, 2 * HEAD_DIM), BF16),
            dma((3,)),
            dma((16,)),
            dma((16,)),
            dma((8,)),
            dma((8,)),
            dma((24,)),
            dma((24,)),
            dma((2,)),
            dma((8,)),
            dma((8,)),
            dma((8,)),
            dma((8,)),
            dma((2,)),
        ],
        compiler_params=pltpu.CompilerParams(
            collective_id=0, has_side_effects=True, vmem_limit_bytes=44 * 2**20
        ),
        cost_estimate=pl.CostEstimate(
            flops=2_500_000_000, bytes_accessed=8_000_000, transcendentals=1_500_000
        ),
        name="gather_project",
    )(vis, w, kvw, mbias, gain, kvbias, cos, sin)


def attention_kernel(count_ref, length_ref, q_ref, tkv_ref, kv_ref, out_ref):
    step = pl.program_id(0)
    live_count = count_ref[0]
    length = length_ref[step]
    keys = jnp.concatenate([kv_ref[:, :HEAD_DIM], tkv_ref[:, :HEAD_DIM]], axis=0)
    values = jnp.concatenate([kv_ref[:, HEAD_DIM:], tkv_ref[:, HEAD_DIM:]], axis=0)
    width = ROWS + RLEN
    values = jnp.concatenate([values, jnp.ones((width, HEAD_DIM), BF16)], axis=1)
    row = lax.broadcasted_iota(jnp.int32, (RLEN, width), 0)
    col = lax.broadcasted_iota(jnp.int32, (RLEN, width), 1)
    live = col < jnp.where(col < ROWS, live_count, row + (ROWS + 1))
    kept = lax.broadcasted_iota(jnp.int32, (RLEN, HEAD_DIM), 0) < length
    factor = HEAD_DIM ** (-0.5) * math.log2(math.e)
    for h in range(8):
        cols = slice(h * HEAD_DIM, (h + 1) * HEAD_DIM)
        scores = lax.dot_general(
            q_ref[:, cols], keys, (((1,), (1,)), ((), ())), preferred_element_type=F32
        )
        scores = jnp.where(live, scores, -1e30)
        highest = jnp.max(scores, axis=1, keepdims=True)
        weights = jnp.exp2((scores - highest) * factor).astype(BF16)
        sums = jnp.dot(weights, values, preferred_element_type=F32)
        attended = sums[:, :HEAD_DIM] / sums[:, HEAD_DIM:]
        out_ref[:, cols] = jnp.where(kept, attended, 0.0).astype(BF16)


def attention(count, length, q, tkv, kv):
    rollouts = length.shape[0]
    return pl.pallas_call(
        attention_kernel,
        grid_spec=pltpu.PrefetchScalarGridSpec(
            num_scalar_prefetch=2,
            grid=(rollouts,),
            in_specs=[
                pl.BlockSpec((RLEN, q.shape[1]), lambda i, *_: (i, 0)),
                pl.BlockSpec((RLEN, tkv.shape[1]), lambda i, *_: (i, 0)),
                pl.BlockSpec(kv.shape, lambda i, *_: (0, 0)),
            ],
            out_specs=pl.BlockSpec((RLEN, q.shape[1]), lambda i, *_: (i, 0)),
        ),
        out_shape=jax.ShapeDtypeStruct(q.shape, BF16),
        compiler_params=pltpu.CompilerParams(vmem_limit_bytes=24 * 2**20),
        name="attention",
    )(count, length, q, tkv, kv)


def rotary_tables(positions):
    half_dim = HEAD_DIM // 2
    inverse = 1000000.0 ** (-jnp.arange(half_dim, dtype=F32) * 2.0 / HEAD_DIM)
    freq_index = jnp.arange(half_dim)
    first_cut = half_dim // 4
    second_cut = first_cut + 3 * half_dim // 8
    pos_f = positions.astype(F32)
    chosen = jnp.where(
        freq_index[None, :] < first_cut,
        pos_f[0][:, None],
        jnp.where(freq_index[None, :] < second_cut, pos_f[1][:, None], pos_f[2][:, None]),
    )
    angles = chosen * inverse
    cosine = jnp.cos(angles)
    sine = jnp.sin(angles)
    return jnp.concatenate([cosine, cosine], axis=1), jnp.concatenate([-sine, sine], axis=1)


def body(
    vis_hidden,
    merge_weight,
    merge_bias,
    norm_gain,
    kv_weight,
    kv_bias,
    queries,
    text_kv,
    image_count,
    image_pos,
    resp_length,
):
    cos, sin = rotary_tables(image_pos)
    kv = gather_project(
        vis_hidden,
        merge_weight,
        kv_weight,
        merge_bias.reshape(1, -1),
        norm_gain.reshape(1, -1),
        kv_bias.reshape(1, -1),
        cos,
        sin,
    )
    return attention(image_count, resp_length, queries, text_kv, kv)


def solution(mesh):
    in_specs = (
        P("group", None),
        P("group", ("roll", "tp")),
        P(("roll", "tp")),
        P(),
        P(None, "tp"),
        P("tp"),
        P(("group", "roll"), "tp"),
        P(("group", "roll"), "tp"),
        P("group"),
        P(None, "group"),
        P(("group", "roll")),
    )
    out_specs = P(("group", "roll"), "tp")
    return jax.shard_map(body, mesh=mesh, in_specs=in_specs, out_specs=out_specs, check_vma=False)
```

time: 199 us -> 89.2 us (0.45)
  the two profiles are of different devices: /device:TPU:6 before, /device:TPU:1 now
where the time goes in v1:
time: 89.2 us; the launch traced here: 88.9 us
  Pallas kernels  79.7 us (89%)
  local copies, waits for them, and re-layouts  7.03 us (8%)
  other arithmetic  1.46 us (2%)
    pallas_call x1, Pallas kernels, gather_project(): pl.pallas_call(gather_project_kernel, out_shape=jax.ShapeDtypeStruct((ROW...  70.3 us
    pallas_call x1, Pallas kernels, attention(): pl.pallas_call(attention_kernel, grid_spec=pltpu.PrefetchScalarGridSpec(n...  9.41 us
    unnamed x18, local copies, waits for them, and re-layouts  7.02 us

profile of v1, /device:TPU:1, one launch (start us, length us, event | category | flops | bytes accessed | tf_op | source)
XLA Modules:
  0.0 88.9 jit_solution(17076733236434980075)
XLA Ops:
  0.7 0.7 convert_element_type.3
  1.4 0.6 fusion.2
  2.0 0.1 pad_maximum_fusion
  2.2 0.0 copy-start.3
  2.2 2.2 %copy-done.3 = bf16[8192,256]{1,0:T(8,128)(2,1)S(1)} copy-done((bf16[8192,256]{1,0:T(8,128)(2,1)S(1)}, bf16[8192,256]{1,0:T(8,128)(2,1)}, u32[]{:S(2)}) %copy-start.3) | copy-done | bytes 4194328
  4.3 0.0 copy-start.4
  4.3 1.7 %copy-done.4 = bf16[256,5120]{1,0:T(8,128)(2,1)S(1)} copy-done((bf16[256,5120]{1,0:T(8,128)(2,1)S(1)}, bf16[256,5120]{1,0:T(8,128)(2,1)}, u32[]{:S(2)}) %copy-start.4) | copy-done | bytes 2621464
  6.1 0.0 copy-start.5
  6.1 1.0 %copy-done.5 = bf16[320,512]{1,0:T(8,128)(2,1)S(1)} copy-done((bf16[320,512]{1,0:T(8,128)(2,1)S(1)}, bf16[320,512]{1,0:T(8,128)(2,1)}, u32[]{:S(2)}) %copy-start.5) | copy-done | bytes 327704
  7.1 0.0 copy-start.6
  7.1 0.8 copy-done.6
  7.8 0.0 copy-start.7
  7.8 0.7 copy-done.7
  8.5 0.0 copy-start.8
  8.5 0.7 copy-done.8
  9.2 0.0 copy-start
  9.2 0.0 copy-start.1
  9.2 0.0 copy-start.2
  9.2 70.3 %gather_project.1.kv_ref = bf16[256,256]{1,0:T(8,128)(2,1)S(1)} custom-call(bf16[256,5120]{1,0:T(8,128)(2,1)S(1)} %copy-done.4, bf16[320,512]{1,0:T(8,128)(2,1)S(1)} %copy-done.5, bf16[8192,256]{1,0:T(8,128)(2,1)S(1)} %copy-done.3, f32[1,512]{1,0:T(1,128)S(1)} %bitcast.7, f32[1,8192]{1,0:T(1,128)S(1)} %bitcast.6, f32[1,256]{1,0:T(1,128)S(1)} %bitcast.8, ...), custom_call_target="tpu_custom_call" | custom-call | flops 2500000000 | bytes 8000000 | tf_op jit(solution)/shard_map/gather_project/pallas_call | solution.py:304
  79.5 0.0 copy-done
  79.5 0.0 copy-done.1
  79.5 0.0 copy-done.2
  79.5 9.4 %attention.1 = bf16[1024,1024]{1,0:T(8,128)(2,1)} custom-call(s32[1]{0:T(128)S(6)} %copy.12.count_ref, s32[8]{0:T(128)S(1)} %copy-done.2, bf16[1024,1024]{1,0:T(8,128)(2,1)S(1)} %copy-done, bf16[1024,256]{1,0:T(8,128)(2,1)S(1)} %copy-done.1, bf16[256,256]{1,0:T(8,128)(2,1)S(1)} %gather_project.1.kv_ref), custom_call_target="tpu_custom_call" | custom-call | tf_op jit(solution)/shard_map/attention/pallas_call | solution.py:376
  (4 shorter events, 0.0 us)
Async XLA Ops:
  2.2 2.2 %copy-start.3 = (bf16[8192,256]{1,0:T(8,128)(2,1)S(1)}, bf16[8192,256]{1,0:T(8,128)(2,1)}, u32[]{:S(2)}) copy-start(bf16[8192,256]{1,0:T(8,128)(2,1)} %kvw_hbm.1) | copy-start | bytes 12582916
  4.3 1.7 %copy-start.4 = (bf16[256,5120]{1,0:T(8,128)(2,1)S(1)}, bf16[256,5120]{1,0:T(8,128)(2,1)}, u32[]{:S(2)}) copy-start(bf16[256,5120]{1,0:T(8,128)(2,1)} %vis_hbm.1) | copy-start | bytes 7864324
  6.1 1.0 %copy-start.5 = (bf16[320,512]{1,0:T(8,128)(2,1)S(1)}, bf16[320,512]{1,0:T(8,128)(2,1)}, u32[]{:S(2)}) copy-start(bf16[320,512]{1,0:T(8,128)(2,1)} %w_hbm.1) | copy-start | bytes 983044
  7.1 0.8 copy-start.6
  7.8 0.7 copy-start.7
  8.5 0.7 copy-start.8
  9.2 70.3 %copy-start = (bf16[1024,1024]{1,0:T(8,128)(2,1)S(1)}, bf16[1024,1024]{1,0:T(8,128)(2,1)}, u32[]{:S(2)}) copy-start(bf16[1024,1024]{1,0:T(8,128)(2,1)} %q_ref.1) | copy-start | bytes 6291460
  9.2 70.3 %copy-start.1 = (bf16[1024,256]{1,0:T(8,128)(2,1)S(1)}, bf16[1024,256]{1,0:T(8,128)(2,1)}, u32[]{:S(2)}) copy-start(bf16[1024,256]{1,0:T(8,128)(2,1)} %tkv_ref.1) | copy-start | bytes 1572868
  9.2 70.3 %copy-start.2 = (s32[8]{0:T(128)S(1)}, s32[8]{0:T(128)}, u32[]{:S(2)}) copy-start(s32[8]{0:T(128)} %length_ref.1) | copy-start | bytes 100

commit v2 on v1

v2 whole, which is shorter than its diff:
```python
import math

import jax
import jax.numpy as jnp
from jax import lax
from jax.experimental import pallas as pl
from jax.experimental.pallas import tpu as pltpu
from jax.sharding import PartitionSpec as P

HEAD_DIM = 128
RLEN = 128
BATCH = 8
UNROLL = 2
MESH = pl.DeviceIdType.MESH
BF16 = jnp.bfloat16
F32 = jnp.float32

ZOFF = (0, 1, -1, 2, -2, 3, -3, 4)
ZBACK = (0, 2, 1, 4, 3, 6, 5, 7)
KVGROUPS = ((0, 3), (3, 2), (5, 3))
SLOTS = [(0, 0), (0, 1), (0, -1), (1, 0), (0, 2), (1, 1), (1, -1), (1, 2)]
NEXT_UP, NEXT_DOWN, CROSS, FAR, CROSS_UP, CROSS_DOWN, CROSS_FAR = range(1, 8)
ROWS = 256
HALF = 128
HID = 320
PAIR = 640
COLS = 512


def gather_project_kernel(
    vis_hbm,
    w_hbm,
    kvw_hbm,
    mbias_hbm,
    gain_hbm,
    kvbias_hbm,
    pos_hbm,
    out_ref,
    mbias_ref,
    gain_ref,
    kvbias_ref,
    pos_ref,
    cos_ref,
    sin_ref,
    vis,
    act,
    wbuf,
    kvbuf,
    acc,
    visual,
    xs,
    xg,
    sumsq,
    sumsq_in,
    sbuf,
    rbuf,
    proj,
    res,
    res_in,
    local_sem,
    w_send,
    w_recv,
    kz_send,
    kz_recv,
    kx_send,
    kx_recv,
    v_sem,
    q_send,
    q_recv,
    p_send,
    p_recv,
    o_sem,
):
    g = lax.axis_index("group")
    roll = lax.axis_index("roll")
    z = lax.axis_index("tp")
    hi = g // 8
    y = lax.rem(g // 2, 4)
    core = lax.rem(g, 2)
    x = 2 * hi + roll
    me_k = hi * 4 + y

    def at(dx=0, dy=0, dz=0, sib=False):
        xx = lax.rem(x + dx + 4, 4)
        yy = lax.rem(y + dy + 4, 4)
        zz = lax.rem(z + dz + 8, 8)
        cc = 1 - core if sib else core
        return ((xx // 2) * 8 + yy * 2 + cc, lax.rem(xx, 2), zz)

    def k_of(dh, dy):
        hh = 1 - hi if dh else hi
        return hh * 4 + lax.rem(y + dy + 4, 4)

    started = []

    def send(src, dst, ssem, rsem, device):
        copy = pltpu.make_async_remote_copy(
            src_ref=src,
            dst_ref=dst,
            send_sem=ssem,
            recv_sem=rsem,
            device_id=device,
            device_id_type=MESH,
        )
        copy.start()
        started.append(copy)

    def arrived(dst, rsem):
        pltpu.make_async_remote_copy(
            src_ref=dst,
            dst_ref=dst,
            send_sem=rsem,
            recv_sem=rsem,
            device_id=at(sib=True),
            device_id_type=MESH,
        ).wait_recv()

    part_start = roll * COLS + core * ROWS

    def kv_piece(first, count, start, rows):
        return kvbuf.at[pl.ds(first, count), pl.ds(pl.multiple_of(start, HALF), rows)]

    def kv_rows(zz):
        start = roll * 4096 + zz * COLS + core * ROWS
        return pl.ds(pl.multiple_of(start, ROWS), ROWS)

    def kv_slot(j):
        return kvbuf.at[j, pl.ds(pl.multiple_of(part_start, ROWS), ROWS)]

    def w_piece(slot, half, cc):
        dh, dy = SLOTS[slot]
        start, rows = (0, HID) if half is None else (half * (HID // 2), HID // 2)
        return wbuf.at[k_of(dh, dy), pl.ds(pl.multiple_of(cc * HID + start, 32), rows)]

    own_w = pltpu.make_async_copy(w_hbm, w_piece(0, None, core), local_sem.at[0])
    own_kv = pltpu.make_async_copy(kvw_hbm.at[kv_rows(z)], kv_slot(0), local_sem.at[1])
    own_vis = pltpu.make_async_copy(vis_hbm, vis, local_sem.at[2])
    own_w.start()
    own_kv.start()
    own_vis.start()
    small = [
        pltpu.make_async_copy(src, dst, local_sem.at[3 + i])
        for i, (src, dst) in enumerate(
            (
                (mbias_hbm, mbias_ref),
                (gain_hbm, gain_ref),
                (kvbias_hbm, kvbias_ref),
                (pos_hbm, pos_ref),
            )
        )
    ]
    for copy in small:
        copy.start()

    partners = [at(dx=1), at(dx=-1), at(dx=2), at(dy=1), at(dy=-1), at(dy=2), at(sib=True)]
    partners += [at(dz=d) for d in ZOFF[1:]]
    barrier = pltpu.get_barrier_semaphore()
    for partner in partners:
        pl.semaphore_signal(barrier, inc=1, device_id=partner, device_id_type=MESH)
    pl.semaphore_wait(barrier, len(partners))

    sent = iter(range(64))
    kx_sent = iter(range(64))

    def w_send_to(slot, half, dx=0, dy=0):
        dh, ddy = SLOTS[slot]
        there = SLOTS.index(((dh + (1 if dx else 0)) % 2, (ddy - dy + 1) % 4 - 1))
        block = w_piece(slot, half, core)
        send(block, block, w_send.at[next(sent)], w_recv.at[there * 2 + half], at(dx=dx, dy=dy))

    def w_wait(slot, half):
        arrived(w_piece(slot, half, core), w_recv.at[slot * 2 + half])

    def w_sibling(slot, half=None):
        block = w_piece(slot, half, core)
        index = 16 + slot * 2 + (half or 0)
        send(block, block, w_send.at[next(sent)], w_recv.at[index], at(sib=True))

    def w_sibling_wait(slot, half=None):
        arrived(w_piece(slot, half, 1 - core), w_recv.at[16 + slot * 2 + (half or 0)])

    own_w.wait()
    for half in (0, 1):
        w_send_to(0, half, dx=2)
    for half in (0, 1):
        w_send_to(0, half, dy=1)
        w_send_to(0, 1 - half, dy=-1)
    for j in (1, 2, 3, 4, 5, 6, 7):
        zz = lax.rem(z + ZOFF[j] + 8, 8)
        send(
            kvw_hbm.at[kv_rows(zz)],
            kv_slot(ZBACK[j]),
            kz_send.at[j],
            kz_recv.at[ZBACK[j]],
            at(dz=ZOFF[j]),
        )
    w_sibling(0)

    own_vis.wait()

    def activate(k):
        def step(i, carry):
            rows = pl.ds(pl.multiple_of(i * 32, 32), 32)
            v = vis[rows, k * PAIR : (k + 1) * PAIR].astype(F32)
            act[k, rows] = (v * (1.0 + lax.erf(v * (1.0 / math.sqrt(2.0)))) * 0.5).astype(BF16)
            return carry

        lax.fori_loop(0, ROWS // 32, step, 0)

    def merge(count, chip):
        def step(i, carry):
            k = chip(i)
            acc[...] += jnp.dot(act[k], wbuf[k], preferred_element_type=F32)
            return carry

        lax.fori_loop(0, count, step, 0)

    def kv_share(group):
        first, count = KVGROUPS[group]
        for j in range(first, first + count):
            if j:
                arrived(kv_slot(j), kz_recv.at[j])
        for i, dx in ((0, 1), (1, -1)):
            block = kv_piece(first, count, part_start + i * HALF, HALF)
            send(block, block, kx_send.at[next(kx_sent)], kx_recv.at[group * 4 + i], at(dx=dx))
        block = kv_piece(first, count, part_start, ROWS)
        send(block, block, kx_send.at[next(kx_sent)], kx_recv.at[group * 4 + 2], at(sib=True))

    other_start = (1 - roll) * COLS + core * ROWS

    def kv_pass(group):
        first, count = KVGROUPS[group]
        for i in (0, 1):
            block = kv_piece(first, count, other_start + i * HALF, HALF)
            arrived(block, kx_recv.at[group * 4 + i])
        block = kv_piece(first, count, other_start, ROWS)
        send(block, block, kx_send.at[next(kx_sent)], kx_recv.at[group * 4 + 3], at(sib=True))

    def kv_end(group):
        first, count = KVGROUPS[group]
        for i, rr in ((2, roll), (3, 1 - roll)):
            block = kv_piece(first, count, rr * COLS + (1 - core) * ROWS, ROWS)
            arrived(block, kx_recv.at[group * 4 + i])

    activate(0)
    activate(1)
    w_wait(NEXT_DOWN, 0)
    w_send_to(NEXT_DOWN, 0, dy=1)
    w_wait(NEXT_UP, 1)
    w_send_to(NEXT_UP, 1, dy=-1)
    activate(2)
    for half in (0, 1):
        w_wait(CROSS, half)
        w_send_to(CROSS, half, dy=1)
        w_send_to(CROSS, half, dy=-1)
        activate(3 + half)
    own_kv.wait()
    kv_share(0)
    w_sibling(CROSS)
    w_wait(NEXT_DOWN, 1)
    w_sibling(NEXT_DOWN)
    w_wait(NEXT_UP, 0)
    w_sibling(NEXT_UP)
    activate(5)
    kv_share(1)
    w_wait(CROSS_DOWN, 0)
    w_send_to(CROSS_DOWN, 0, dy=1)
    w_wait(CROSS_UP, 1)
    w_send_to(CROSS_UP, 1, dy=-1)
    activate(6)
    for half in (0, 1):
        w_wait(FAR, half)
    w_sibling(FAR)
    kv_share(2)
    activate(7)
    for copy in small:
        copy.wait()
    mine = pl.ds(pl.multiple_of(roll * HALF, HALF), HALF)
    theirs = pl.ds(pl.multiple_of((1 - roll) * HALF, HALF), HALF)
    lane = lax.broadcasted_iota(jnp.int32, (HALF, HEAD_DIM), 1)
    freq = lax.rem(lane, HEAD_DIM // 2)
    pos = pos_ref[:, mine].astype(F32)
    by_row = [jnp.broadcast_to(pos[s : s + 1], (HALF, HEAD_DIM)).T for s in range(3)]
    chosen = jnp.where(freq < 16, by_row[0], jnp.where(freq < 40, by_row[1], by_row[2]))
    angle = chosen * jnp.exp(freq.astype(F32) * (-2.0 * math.log(1e6) / HEAD_DIM))
    sine = jnp.sin(angle)
    cos_ref[...] = jnp.cos(angle)
    sin_ref[...] = jnp.where(lane < HEAD_DIM // 2, -sine, sine)

    acc[...] = jnp.broadcast_to(mbias_ref[...], acc.shape)
    kv_pass(0)
    w_wait(CROSS_DOWN, 1)
    w_sibling(CROSS_DOWN)
    w_wait(CROSS_UP, 0)
    w_sibling(CROSS_UP)
    for slot in (0, NEXT_DOWN, NEXT_UP, FAR):
        w_sibling_wait(slot)
    merge(4, lambda i: hi * 4 + i)
    kv_pass(1)
    for half in (0, 1):
        w_wait(CROSS_FAR, half)
        w_sibling(CROSS_FAR, half)
    for slot in (CROSS, CROSS_DOWN, CROSS_UP):
        w_sibling_wait(slot)
    merge(3, lambda i: (1 - hi) * 4 + lax.rem(y + i + 3, 4))
    kv_pass(2)
    for half in (0, 1):
        w_sibling_wait(CROSS_FAR, half)
    merge(1, lambda i: (1 - hi) * 4 + lax.rem(y + 2, 4))

    visual[...] = acc[...].astype(BF16)
    partner = (g, 1 - roll, z)
    send(visual.at[theirs], xs.at[roll], v_sem.at[0], v_sem.at[1], partner)
    xs[roll] = visual[mine, :]
    for group in range(3):
        kv_end(group)
    arrived(xs.at[1 - roll], v_sem.at[1])

    total = jnp.zeros((HALF, 1), F32)
    for r in range(2):
        start = pl.multiple_of(r * 4096 + z * COLS, COLS)
        v = xs[r].astype(F32)
        total += jnp.sum(v * v, axis=1, keepdims=True)
        xg[r] = (v * gain_ref[:, pl.ds(start, COLS)]).astype(BF16)
    sumsq[...] = jnp.broadcast_to(total, (HALF, HALF)).T[:8]

    def product(j):
        return jnp.dot(xg[0], kvbuf[j, :COLS], preferred_element_type=F32) + jnp.dot(
            xg[1], kvbuf[j, COLS:], preferred_element_type=F32
        )

    def partial_copies(j):
        sign = 2 * lax.rem(j, 2) - 1
        device = at(dz=(j + 1) // 2 * sign)
        back = j + sign * (1 - j // 7)
        return [
            pltpu.make_async_remote_copy(
                src_ref=src,
                dst_ref=dst.at[back],
                send_sem=ssem.at[j],
                recv_sem=rsem.at[back],
                device_id=device,
                device_id_type=MESH,
            )
            for src, dst, ssem, rsem in (
                (sumsq, sumsq_in, q_send, q_recv),
                (sbuf.at[j], rbuf, p_send, p_recv),
            )
        ]

    def partial_step(i, carry):
        j = 7 - i
        copies = partial_copies(j)
        copies[0].start()
        sbuf[j] = product(j).astype(BF16)
        copies[1].start()
        return carry

    lax.fori_loop(0, 7, partial_step, 0)
    proj[...] = product(0)

    def total_step(j, square):
        arrived(sumsq_in.at[j], q_recv.at[j])
        arrived(rbuf.at[j], p_recv.at[j])
        proj[...] += rbuf[j].astype(F32)
        return square + sumsq_in[j]

    square = lax.fori_loop(1, 8, total_step, sumsq[...])
    inv = lax.rsqrt(square * (1.0 / 8192.0) + 1e-06)
    inv = jnp.broadcast_to(inv[:1], (HALF, HALF)).T
    key = proj[:, :HEAD_DIM] * inv + kvbias_ref[:, :HEAD_DIM]
    value = proj[:, HEAD_DIM:] * inv + kvbias_ref[:, HEAD_DIM:]
    key = key * cos_ref[...] + pltpu.roll(key, HEAD_DIM // 2, 1) * sin_ref[...]
    res[:, :HEAD_DIM] = key.astype(BF16)
    res[:, HEAD_DIM:] = value.astype(BF16)
    send(res, res_in, o_sem.at[0], o_sem.at[1], partner)
    out_ref[mine, :] = res[...]
    arrived(res_in, o_sem.at[1])
    out_ref[theirs, :] = res_in[...]
    for copy in started:
        copy.wait_send()

    def sent_step(j, carry):
        for copy in partial_copies(j):
            copy.wait_send()
        return carry

    lax.fori_loop(1, 8, sent_step, 0)


def gather_project(vis, w, kvw, mbias, gain, kvbias, pos):
    vmem = pl.BlockSpec(memory_space=pltpu.VMEM)
    hbm = pl.BlockSpec(memory_space=pltpu.HBM)
    dma = pltpu.SemaphoreType.DMA
    return pl.pallas_call(
        gather_project_kernel,
        out_shape=jax.ShapeDtypeStruct((ROWS, 2 * HEAD_DIM), BF16),
        in_specs=[hbm] * 7,
        out_specs=vmem,
        scratch_shapes=[
            pltpu.VMEM((1, COLS), F32),
            pltpu.VMEM((1, 8192), F32),
            pltpu.VMEM((1, 2 * HEAD_DIM), F32),
            pltpu.VMEM((3, ROWS), jnp.int32),
            pltpu.VMEM((HALF, HEAD_DIM), F32),
            pltpu.VMEM((HALF, HEAD_DIM), F32),
            pltpu.VMEM((ROWS, 5120), BF16),
            pltpu.VMEM((8, ROWS, PAIR), BF16),
            pltpu.VMEM((8, PAIR, COLS), BF16),
            pltpu.VMEM((8, 1024, 2 * HEAD_DIM), BF16),
            pltpu.VMEM((ROWS, COLS), F32),
            pltpu.VMEM((ROWS, COLS), BF16),
            pltpu.VMEM((2, HALF, COLS), BF16),
            pltpu.VMEM((2, HALF, COLS), BF16),
            pltpu.VMEM((8, HALF), F32),
            pltpu.VMEM((8, 8, HALF), F32),
            pltpu.VMEM((8, HALF, 2 * HEAD_DIM), BF16),
            pltpu.VMEM((8, HALF, 2 * HEAD_DIM), BF16),
            pltpu.VMEM((HALF, 2 * HEAD_DIM), F32),
            pltpu.VMEM((HALF, 2 * HEAD_DIM), BF16),
            pltpu.VMEM((HALF, 2 * HEAD_DIM), BF16),
            dma((7,)),
            dma((32,)),
            dma((32,)),
            dma((8,)),
            dma((8,)),
            dma((12,)),
            dma((12,)),
            dma((2,)),
            dma((8,)),
            dma((8,)),
            dma((8,)),
            dma((8,)),
            dma((2,)),
        ],
        compiler_params=pltpu.CompilerParams(
            collective_id=0, has_side_effects=True, vmem_limit_bytes=64 * 2**20
        ),
        cost_estimate=pl.CostEstimate(
            flops=2_500_000_000, bytes_accessed=8_000_000, transcendentals=1_500_000
        ),
        name="gather_project",
    )(vis, w, kvw, mbias, gain, kvbias, pos)


def attention_kernel(
    count_ref,
    length_ref,
    q_hbm,
    tkv_hbm,
    kv_hbm,
    out_hbm,
    q_in,
    tkv_in,
    kv_in,
    out,
    keys,
    values,
    kv_sem,
    tkv_sem,
    q_sem,
    out_sem,
):
    rollouts = q_in.shape[0]
    kv_copy = pltpu.make_async_copy(kv_hbm, kv_in, kv_sem)
    kv_copy.start()

    def load(r, carry):
        rows = pl.ds(pl.multiple_of(r * RLEN, RLEN), RLEN)
        pltpu.make_async_copy(tkv_hbm.at[rows], tkv_in.at[r], tkv_sem.at[r]).start()
        pltpu.make_async_copy(q_hbm.at[rows], q_in.at[r], q_sem.at[r]).start()
        return carry

    lax.fori_loop(0, rollouts, load, 0)

    kv_copy.wait()
    live = lax.broadcasted_iota(jnp.int32, (ROWS, HEAD_DIM), 0) < count_ref[0]
    image_keys = kv_in[:, :HEAD_DIM]
    image_keys = jnp.where(live, image_keys, image_keys[:1])
    image_values = jnp.where(live, kv_in[:, HEAD_DIM:], 0.0).astype(BF16)
    keys[...] = image_keys
    values[:, :HEAD_DIM] = image_values
    values[:, HEAD_DIM:] = jnp.where(live, 1.0, 0.0).astype(BF16)

    batch = BATCH * RLEN
    token = lax.rem(lax.broadcasted_iota(jnp.int32, (batch, RLEN), 0), RLEN)
    causal = lax.broadcasted_iota(jnp.int32, (batch, RLEN), 1) <= token
    factor = HEAD_DIM ** (-0.5) * math.log2(math.e)
    def one(r):
        rows = pl.ds(pl.multiple_of(r * RLEN, RLEN), RLEN)
        text_keys = tkv_in[r, :, :HEAD_DIM]
        text_values = jnp.concatenate(
            [tkv_in[r, :, HEAD_DIM:], jnp.ones((RLEN, HEAD_DIM), BF16)], axis=1
        )
        kept = token < length_ref[r]
        for h in range(0, 8, BATCH):
            heads = [slice(k * HEAD_DIM, (k + 1) * HEAD_DIM) for k in range(h, h + BATCH)]
            q = jnp.concatenate([q_in[r, :, cols] for cols in heads], axis=0)
            image = lax.dot_general(
                q, keys[...], (((1,), (1,)), ((), ())), preferred_element_type=F32
            )
            text = lax.dot_general(
                q, text_keys, (((1,), (1,)), ((), ())), preferred_element_type=F32
            )
            text = jnp.where(causal, text, -1e30)
            highest = jnp.maximum(
                jnp.maximum(image[:, :HEAD_DIM], image[:, HEAD_DIM:]), text
            )
            highest = jnp.max(highest, axis=1, keepdims=True)
            image = jnp.exp2((image - highest) * factor).astype(BF16)
            text = jnp.exp2((text - highest) * factor).astype(BF16)
            sums = jnp.dot(image, values[...], preferred_element_type=F32)
            sums += jnp.dot(text, text_values, preferred_element_type=F32)
            attended = jnp.where(kept, sums[:, :HEAD_DIM] / sums[:, HEAD_DIM:], 0.0).astype(BF16)
            for i, cols in enumerate(heads):
                out[r, :, cols] = attended[i * RLEN : (i + 1) * RLEN]

    def rollout(step, carry):
        for i in range(UNROLL):
            r = step * UNROLL + i
            rows = pl.ds(pl.multiple_of(r * RLEN, RLEN), RLEN)
            pltpu.make_async_copy(tkv_hbm.at[rows], tkv_in.at[r], tkv_sem.at[r]).wait()
            pltpu.make_async_copy(q_hbm.at[rows], q_in.at[r], q_sem.at[r]).wait()
        for i in range(UNROLL):
            one(step * UNROLL + i)
        for i in range(UNROLL):
            r = step * UNROLL + i
            rows = pl.ds(pl.multiple_of(r * RLEN, RLEN), RLEN)
            pltpu.make_async_copy(out.at[r], out_hbm.at[rows], out_sem.at[r]).start()
        return carry

    lax.fori_loop(0, rollouts // UNROLL, rollout, 0)

    def stored(r, carry):
        rows = pl.ds(pl.multiple_of(r * RLEN, RLEN), RLEN)
        pltpu.make_async_copy(out.at[r], out_hbm.at[rows], out_sem.at[r]).wait()
        return carry

    lax.fori_loop(0, rollouts, stored, 0)


def attention(count, length, q, tkv, kv):
    rollouts = length.shape[0]
    smem = pl.BlockSpec(memory_space=pltpu.SMEM)
    hbm = pl.BlockSpec(memory_space=pl.ANY)
    dma = pltpu.SemaphoreType.DMA
    return pl.pallas_call(
        attention_kernel,
        in_specs=[smem, smem, hbm, hbm, hbm],
        out_specs=hbm,
        out_shape=jax.ShapeDtypeStruct(q.shape, BF16),
        scratch_shapes=[
            pltpu.VMEM((rollouts, RLEN, q.shape[1]), BF16),
            pltpu.VMEM((rollouts, RLEN, tkv.shape[1]), BF16),
            pltpu.VMEM(kv.shape, BF16),
            pltpu.VMEM((rollouts, RLEN, q.shape[1]), BF16),
            pltpu.VMEM((ROWS, HEAD_DIM), BF16),
            pltpu.VMEM((ROWS, 2 * HEAD_DIM), BF16),
            dma,
            dma((rollouts,)),
            dma((rollouts,)),
            dma((rollouts,)),
        ],
        compiler_params=pltpu.CompilerParams(vmem_limit_bytes=64 * 2**20),
        name="attention",
    )(count, length, q, tkv, kv)


def body(
    vis_hidden,
    merge_weight,
    merge_bias,
    norm_gain,
    kv_weight,
    kv_bias,
    queries,
    text_kv,
    image_count,
    image_pos,
    resp_length,
):
    kv = gather_project(
        vis_hidden,
        merge_weight,
        kv_weight,
        merge_bias.reshape(1, -1),
        norm_gain.reshape(1, -1),
        kv_bias.reshape(1, -1),
        image_pos,
    )
    return attention(image_count, resp_length, queries, text_kv, kv)


def solution(mesh):
    in_specs = (
        P("group", None),
        P("group", ("roll", "tp")),
        P(("roll", "tp")),
        P(),
        P(None, "tp"),
        P("tp"),
        P(("group", "roll"), "tp"),
        P(("group", "roll"), "tp"),
        P("group"),
        P(None, "group"),
        P(("group", "roll")),
    )
    out_specs = P(("group", "roll"), "tp")
    return jax.shard_map(body, mesh=mesh, in_specs=in_specs, out_specs=out_specs, check_vma=False)
```

time: 89.2 us -> 72.3 us (0.81)
  the two profiles are of different devices: /device:TPU:1 before, /device:TPU:22 now
where the time goes in v2:
time: 72.3 us; the launch traced here: 72.2 us
  Pallas kernels  71.5 us (99%)
    pallas_call x1, Pallas kernels, gather_project(): pl.pallas_call(gather_project_kernel, out_shape=jax.ShapeDtypeStruct((ROW...  63.2 us
    pallas_call x1, Pallas kernels, attention(): pl.pallas_call(attention_kernel, in_specs=[smem, smem, hbm, hbm, hbm], ou...  8.35 us

profile of v2, /device:TPU:22, one launch (start us, length us, event | category | flops | bytes accessed | tf_op | source)
XLA Modules:
  0.0 72.2 jit_solution(17451022299129457097)
XLA Ops:
  0.7 63.2 %gather_project.1.kv_hbm = bf16[256,256]{1,0:T(8,128)(2,1)} custom-call(bf16[256,5120]{1,0:T(8,128)(2,1)} %vis_hbm.1, bf16[320,512]{1,0:T(8,128)(2,1)} %w_hbm.1, bf16[8192,256]{1,0:T(8,128)(2,1)} %kvw_hbm.1, f32[1,512]{1,0:T(1,128)} %bitcast.4, f32[1,8192]{1,0:T(1,128)} %bitcast.3, f32[1,256]{1,0:T(1,128)} %bitcast.5, s32[3,256]{1,0:T(4,128)} %pos_hbm.1), custom_call_target="tpu_custom_call" | custom-call | flops 2500000000 | bytes 8000000 | tf_op jit(solution)/shard_map/gather_project/pallas_call | solution.py:395
  63.8 8.3 %attention.1 = bf16[1024,1024]{1,0:T(8,128)(2,1)} custom-call(s32[1]{0:T(128)S(6)} %copy.12.count_ref, s32[8]{0:T(128)} %length_ref.1, bf16[1024,1024]{1,0:T(8,128)(2,1)} %q_hbm.1, bf16[1024,256]{1,0:T(8,128)(2,1)} %tkv_hbm.1, bf16[256,256]{1,0:T(8,128)(2,1)} %gather_project.1.kv_hbm), custom_call_target="tpu_custom_call" | custom-call | tf_op jit(solution)/shard_map/attention/pallas_call | solution.py:547

commit v3 on v2

--- a/solution.py
+++ b/solution.py
@@ -10,14 +10,15 @@
 HEAD_DIM = 128
 RLEN = 128
 BATCH = 8
-UNROLL = 2
+UNROLL = 4
 MESH = pl.DeviceIdType.MESH
 BF16 = jnp.bfloat16
 F32 = jnp.float32
 
 ZOFF = (0, 1, -1, 2, -2, 3, -3, 4)
 ZBACK = (0, 2, 1, 4, 3, 6, 5, 7)
-KVGROUPS = ((0, 3), (3, 2), (5, 3))
+KVGROUPS = ((0, 3), (3, 2), (5, 2))
+FAR_SLOT = 7
 SLOTS = [(0, 0), (0, 1), (0, -1), (1, 0), (0, 2), (1, 1), (1, -1), (1, 2)]
 NEXT_UP, NEXT_DOWN, CROSS, FAR, CROSS_UP, CROSS_DOWN, CROSS_FAR = range(1, 8)
 ROWS = 256
@@ -124,6 +125,15 @@
         start = roll * 4096 + zz * COLS + core * ROWS
         return pl.ds(pl.multiple_of(start, ROWS), ROWS)
 
+    quarter = x * 2 + core
+
+    def far_rows(zz):
+        start = (quarter // 4) * 4096 + zz * COLS + lax.rem(quarter, 4) * HALF
+        return pl.ds(pl.multiple_of(start, HALF), HALF)
+
+    def far_piece(part):
+        return kvbuf.at[FAR_SLOT, pl.ds(pl.multiple_of(part * HALF, HALF), HALF)]
+
     def kv_slot(j):
         return kvbuf.at[j, pl.ds(pl.multiple_of(part_start, ROWS), ROWS)]
 
@@ -182,10 +192,7 @@
     own_w.wait()
     for half in (0, 1):
         w_send_to(0, half, dx=2)
-    for half in (0, 1):
-        w_send_to(0, half, dy=1)
-        w_send_to(0, 1 - half, dy=-1)
-    for j in (1, 2, 3, 4, 5, 6, 7):
+    for j in (1, 2, 3, 4, 5, 6):
         zz = lax.rem(z + ZOFF[j] + 8, 8)
         send(
             kvw_hbm.at[kv_rows(zz)],
@@ -194,6 +201,16 @@
             kz_recv.at[ZBACK[j]],
             at(dz=ZOFF[j]),
         )
+    send(
+        kvw_hbm.at[far_rows(lax.rem(z + 4, 8))],
+        far_piece(quarter),
+        kz_send.at[FAR_SLOT],
+        kz_recv.at[FAR_SLOT],
+        at(dz=4),
+    )
+    for half in (0, 1):
+        w_send_to(0, half, dy=1)
+        w_send_to(0, 1 - half, dy=-1)
     w_sibling(0)
 
     own_vis.wait()
@@ -235,6 +252,29 @@
             arrived(block, kx_recv.at[group * 4 + i])
         block = kv_piece(first, count, other_start, ROWS)
         send(block, block, kx_send.at[next(kx_sent)], kx_recv.at[group * 4 + 3], at(sib=True))
+
+    far_sources = ((1, 13), (-1, 14), (2, 15))
+
+    def far_at(dx, cc):
+        return far_piece(lax.rem(x + dx + 4, 4) * 2 + cc)
+
+    def far_share():
+        block = far_piece(quarter)
+        arrived(block, kz_recv.at[FAR_SLOT])
+        for dx, index in ((2, 15), (1, 14), (-1, 13)):
+            send(block, block, kx_send.at[next(kx_sent)], kx_recv.at[index], at(dx=dx))
+        send(block, block, kx_send.at[next(kx_sent)], kx_recv.at[12], at(sib=True))
+
+    def far_pass():
+        for dx, index in far_sources:
+            block = far_at(dx, core)
+            arrived(block, kx_recv.at[index])
+            send(block, block, kx_send.at[next(kx_sent)], kx_recv.at[index + 3], at(sib=True))
+
+    def far_end():
+        arrived(far_at(0, 1 - core), kx_recv.at[12])
+        for dx, index in far_sources:
+            arrived(far_at(dx, 1 - core), kx_recv.at[index + 3])
 
     def kv_end(group):
         first, count = KVGROUPS[group]
@@ -272,6 +312,7 @@
         w_wait(FAR, half)
     w_sibling(FAR)
     kv_share(2)
+    far_share()
     activate(7)
     for copy in small:
         copy.wait()
@@ -304,6 +345,7 @@
         w_sibling_wait(slot)
     merge(3, lambda i: (1 - hi) * 4 + lax.rem(y + i + 3, 4))
     kv_pass(2)
+    far_pass()
     for half in (0, 1):
         w_sibling_wait(CROSS_FAR, half)
     merge(1, lambda i: (1 - hi) * 4 + lax.rem(y + 2, 4))
@@ -314,6 +356,7 @@
     xs[roll] = visual[mine, :]
     for group in range(3):
         kv_end(group)
+    far_end()
     arrived(xs.at[1 - roll], v_sem.at[1])
 
     total = jnp.zeros((HALF, 1), F32)
@@ -329,45 +372,65 @@
             xg[1], kvbuf[j, COLS:], preferred_element_type=F32
         )
 
-    def partial_copies(j):
+    def sumsq_copy(j):
         sign = 2 * lax.rem(j, 2) - 1
-        device = at(dz=(j + 1) // 2 * sign)
         back = j + sign * (1 - j // 7)
-        return [
-            pltpu.make_async_remote_copy(
-                src_ref=src,
-                dst_ref=dst.at[back],
-                send_sem=ssem.at[j],
-                recv_sem=rsem.at[back],
-                device_id=device,
-                device_id_type=MESH,
-            )
-            for src, dst, ssem, rsem in (
-                (sumsq, sumsq_in, q_send, q_recv),
-                (sbuf.at[j], rbuf, p_send, p_recv),
-            )
-        ]
-
-    def partial_step(i, carry):
-        j = 7 - i
-        copies = partial_copies(j)
-        copies[0].start()
-        sbuf[j] = product(j).astype(BF16)
-        copies[1].start()
+        return pltpu.make_async_remote_copy(
+            src_ref=sumsq,
+            dst_ref=sumsq_in.at[back],
+            send_sem=q_send.at[j],
+            recv_sem=q_recv.at[back],
+            device_id=at(dz=(j + 1) // 2 * sign),
+            device_id_type=MESH,
+        )
+
+    def sumsq_send(i, carry):
+        sumsq_copy(i).start()
         return carry
 
-    lax.fori_loop(0, 7, partial_step, 0)
+    lax.fori_loop(1, 8, sumsq_send, 0)
+
+    way = 1 - 2 * core
+
+    def ahead(k):
+        return 2 * k - 1 + core
+
+    def behind(k):
+        return 2 * k - core
+
+    def partial_send(j, dst, slot, steps):
+        send(sbuf.at[j], dst.at[slot], p_send.at[j], p_recv.at[slot], at(dz=way * steps))
+
+    sbuf[7] = product(7).astype(BF16)
+    partial_send(7, rbuf, 7, 1)
+    sbuf[behind(3)] = product(behind(3)).astype(BF16)
+    partial_send(behind(3), rbuf, 0, -1)
+    sbuf[ahead(2)] = product(ahead(2)).astype(BF16)
+    partial_send(ahead(2), rbuf, behind(2), 2)
+    sbuf[ahead(1)] = product(ahead(1)).astype(BF16)
+    partial_send(ahead(1), rbuf, behind(1), 1)
+    sbuf[behind(1)] = product(behind(1)).astype(BF16)
+    partial_send(behind(1), rbuf, ahead(1), -1)
+    proj[...] = product(ahead(3))
+    arrived(rbuf.at[7], p_recv.at[7])
+    sbuf[ahead(3)] = (proj[...] + rbuf[7].astype(F32)).astype(BF16)
+    partial_send(ahead(3), rbuf, behind(3), 3)
+    proj[...] = product(behind(2))
+    arrived(rbuf.at[0], p_recv.at[0])
+    sbuf[behind(2)] = (proj[...] + rbuf[0].astype(F32)).astype(BF16)
+    partial_send(behind(2), rbuf, ahead(2), -2)
     proj[...] = product(0)
 
-    def total_step(j, square):
+    def square_step(j, square):
         arrived(sumsq_in.at[j], q_recv.at[j])
-        arrived(rbuf.at[j], p_recv.at[j])
-        proj[...] += rbuf[j].astype(F32)
         return square + sumsq_in[j]
 
-    square = lax.fori_loop(1, 8, total_step, sumsq[...])
+    square = lax.fori_loop(1, 8, square_step, sumsq[...])
     inv = lax.rsqrt(square * (1.0 / 8192.0) + 1e-06)
     inv = jnp.broadcast_to(inv[:1], (HALF, HALF)).T
+    for slot in (ahead(1), behind(1), behind(2), ahead(2), behind(3)):
+        arrived(rbuf.at[slot], p_recv.at[slot])
+        proj[...] += rbuf[slot].astype(F32)
     key = proj[:, :HEAD_DIM] * inv + kvbias_ref[:, :HEAD_DIM]
     value = proj[:, HEAD_DIM:] * inv + kvbias_ref[:, HEAD_DIM:]
     key = key * cos_ref[...] + pltpu.roll(key, HEAD_DIM // 2, 1) * sin_ref[...]
@@ -381,8 +444,7 @@
         copy.wait_send()
 
     def sent_step(j, carry):
-        for copy in partial_copies(j):
-            copy.wait_send()
+        sumsq_copy(j).wait_send()
         return carry
 
     lax.fori_loop(1, 8, sent_step, 0)
@@ -424,8 +486,8 @@
             dma((32,)),
             dma((8,)),
             dma((8,)),
-            dma((12,)),
-            dma((12,)),
+            dma((19,)),
+            dma((19,)),
             dma((2,)),
             dma((8,)),
             dma((8,)),
@@ -434,7 +496,7 @@
             dma((2,)),
         ],
         compiler_params=pltpu.CompilerParams(
-            collective_id=0, has_side_effects=True, vmem_limit_bytes=64 * 2**20
+            collective_id=0, has_side_effects=True, vmem_limit_bytes=60 * 2**20
         ),
         cost_estimate=pl.CostEstimate(
             flops=2_500_000_000, bytes_accessed=8_000_000, transcendentals=1_500_000
@@ -446,34 +508,16 @@
 def attention_kernel(
     count_ref,
     length_ref,
-    q_hbm,
-    tkv_hbm,
-    kv_hbm,
-    out_hbm,
     q_in,
     tkv_in,
     kv_in,
+    out_hbm,
     out,
     keys,
     values,
-    kv_sem,
-    tkv_sem,
-    q_sem,
     out_sem,
 ):
-    rollouts = q_in.shape[0]
-    kv_copy = pltpu.make_async_copy(kv_hbm, kv_in, kv_sem)
-    kv_copy.start()
-
-    def load(r, carry):
-        rows = pl.ds(pl.multiple_of(r * RLEN, RLEN), RLEN)
-        pltpu.make_async_copy(tkv_hbm.at[rows], tkv_in.at[r], tkv_sem.at[r]).start()
-        pltpu.make_async_copy(q_hbm.at[rows], q_in.at[r], q_sem.at[r]).start()
-        return carry
-
-    lax.fori_loop(0, rollouts, load, 0)
-
-    kv_copy.wait()
+    rollouts = length_ref.shape[0]
     live = lax.broadcasted_iota(jnp.int32, (ROWS, HEAD_DIM), 0) < count_ref[0]
     image_keys = kv_in[:, :HEAD_DIM]
     image_keys = jnp.where(live, image_keys, image_keys[:1])
@@ -488,14 +532,14 @@
     factor = HEAD_DIM ** (-0.5) * math.log2(math.e)
     def one(r):
         rows = pl.ds(pl.multiple_of(r * RLEN, RLEN), RLEN)
-        text_keys = tkv_in[r, :, :HEAD_DIM]
+        text_keys = tkv_in[rows, :HEAD_DIM]
         text_values = jnp.concatenate(
-            [tkv_in[r, :, HEAD_DIM:], jnp.ones((RLEN, HEAD_DIM), BF16)], axis=1
+            [tkv_in[rows, HEAD_DIM:], jnp.ones((RLEN, HEAD_DIM), BF16)], axis=1
         )
         kept = token < length_ref[r]
         for h in range(0, 8, BATCH):
             heads = [slice(k * HEAD_DIM, (k + 1) * HEAD_DIM) for k in range(h, h + BATCH)]
-            q = jnp.concatenate([q_in[r, :, cols] for cols in heads], axis=0)
+            q = jnp.concatenate([q_in[rows, cols] for cols in heads], axis=0)
             image = lax.dot_general(
                 q, keys[...], (((1,), (1,)), ((), ())), preferred_element_type=F32
             )
@@ -517,11 +561,6 @@
 
     def rollout(step, carry):
         for i in range(UNROLL):
-            r = step * UNROLL + i
-            rows = pl.ds(pl.multiple_of(r * RLEN, RLEN), RLEN)
-            pltpu.make_async_copy(tkv_hbm.at[rows], tkv_in.at[r], tkv_sem.at[r]).wait()
-            pltpu.make_async_copy(q_hbm.at[rows], q_in.at[r], q_sem.at[r]).wait()
-        for i in range(UNROLL):
             one(step * UNROLL + i)
         for i in range(UNROLL):
             r = step * UNROLL + i
@@ -542,26 +581,21 @@
 def attention(count, length, q, tkv, kv):
     rollouts = length.shape[0]
     smem = pl.BlockSpec(memory_space=pltpu.SMEM)
+    vmem = pl.BlockSpec(memory_space=pltpu.VMEM)
     hbm = pl.BlockSpec(memory_space=pl.ANY)
     dma = pltpu.SemaphoreType.DMA
     return pl.pallas_call(
         attention_kernel,
-        in_specs=[smem, smem, hbm, hbm, hbm],
+        in_specs=[smem, smem, vmem, vmem, vmem],
         out_specs=hbm,
         out_shape=jax.ShapeDtypeStruct(q.shape, BF16),
         scratch_shapes=[
             pltpu.VMEM((rollouts, RLEN, q.shape[1]), BF16),
-            pltpu.VMEM((rollouts, RLEN, tkv.shape[1]), BF16),
-            pltpu.VMEM(kv.shape, BF16),
-            pltpu.VMEM((rollouts, RLEN, q.shape[1]), BF16),
             pltpu.VMEM((ROWS, HEAD_DIM), BF16),
             pltpu.VMEM((ROWS, 2 * HEAD_DIM), BF16),
-            dma,
-            dma((rollouts,)),
-            dma((rollouts,)),
             dma((rollouts,)),
         ],
-        compiler_params=pltpu.CompilerParams(vmem_limit_bytes=64 * 2**20),
+        compiler_params=pltpu.CompilerParams(vmem_limit_bytes=32 * 2**20),
         name="attention",
     )(count, length, q, tkv, kv)
 

time: 72.3 us -> 66.5 us (0.920)
  the two profiles are of different devices: /device:TPU:22 before, /device:TPU:6 now
where the time goes in v3:
time: 66.5 us; the launch traced here: 66.4 us
  Pallas kernels  64.8 us (97%)
  local copies, waits for them, and re-layouts  0.91 us (1%)
  between operations  0.72 us (1%)
    pallas_call x1, Pallas kernels, gather_project(): pl.pallas_call(gather_project_kernel, out_shape=jax.ShapeDtypeStruct((ROW...  58 us
    pallas_call x1, Pallas kernels, attention(): pl.pallas_call(attention_kernel, in_specs=[smem, smem, vmem, vmem, vmem],...  6.77 us

profile of v3, /device:TPU:6, one launch (start us, length us, event | category | flops | bytes accessed | tf_op | source)
XLA Modules:
  0.0 66.4 jit_solution(2752061023277941876)
XLA Ops:
  0.7 0.0 copy-start
  0.7 0.0 copy-start.1
  0.7 0.0 copy-start.3
  0.7 58.0 %gather_project.1.kv_in = bf16[256,256]{1,0:T(8,128)(2,1)} custom-call(bf16[256,5120]{1,0:T(8,128)(2,1)} %vis_hbm.1, bf16[320,512]{1,0:T(8,128)(2,1)} %w_hbm.1, bf16[8192,256]{1,0:T(8,128)(2,1)} %kvw_hbm.1, f32[1,512]{1,0:T(1,128)} %bitcast.4, f32[1,8192]{1,0:T(1,128)} %bitcast.3, f32[1,256]{1,0:T(1,128)} %bitcast.5, s32[3,256]{1,0:T(4,128)} %pos_hbm.1), custom_call_target="tpu_custom_call" | custom-call | flops 2500000000 | bytes 8000000 | tf_op jit(solution)/shard_map/gather_project/pallas_call | solution.py:457
  58.7 0.0 copy-done
  58.7 0.0 copy-done.1
  58.8 0.0 copy-done.3
  58.8 0.0 copy-start.2
  58.8 0.9 %copy-done.2 = bf16[256,256]{1,0:T(8,128)(2,1)S(1)} copy-done((bf16[256,256]{1,0:T(8,128)(2,1)S(1)}, bf16[256,256]{1,0:T(8,128)(2,1)}, u32[]{:S(2)}) %copy-start.2) | copy-done | bytes 131096
  59.7 6.8 %attention.1 = bf16[1024,1024]{1,0:T(8,128)(2,1)} custom-call(s32[1]{0:T(128)S(6)} %copy.12.count_ref, s32[8]{0:T(128)S(1)} %copy-done.3, bf16[1024,1024]{1,0:T(8,128)(2,1)S(1)} %copy-done, bf16[1024,256]{1,0:T(8,128)(2,1)S(1)} %copy-done.1, bf16[256,256]{1,0:T(8,128)(2,1)S(1)} %copy-done.2), custom_call_target="tpu_custom_call" | custom-call | tf_op jit(solution)/shard_map/attention/pallas_call | solution.py:587
Async XLA Ops:
  0.7 58.1 %copy-start = (bf16[1024,1024]{1,0:T(8,128)(2,1)S(1)}, bf16[1024,1024]{1,0:T(8,128)(2,1)}, u32[]{:S(2)}) copy-start(bf16[1024,1024]{1,0:T(8,128)(2,1)} %q_in.1) | copy-start | bytes 6291460
  0.7 58.1 %copy-start.1 = (bf16[1024,256]{1,0:T(8,128)(2,1)S(1)}, bf16[1024,256]{1,0:T(8,128)(2,1)}, u32[]{:S(2)}) copy-start(bf16[1024,256]{1,0:T(8,128)(2,1)} %tkv_in.1) | copy-start | bytes 1572868
  0.7 58.1 %copy-start.3 = (s32[8]{0:T(128)S(1)}, s32[8]{0:T(128)}, u32[]{:S(2)}) copy-start(s32[8]{0:T(128)} %length_ref.1) | copy-start | bytes 100
  58.8 0.9 %copy-start.2 = (bf16[256,256]{1,0:T(8,128)(2,1)S(1)}, bf16[256,256]{1,0:T(8,128)(2,1)}, u32[]{:S(2)}) copy-start(bf16[256,256]{1,0:T(8,128)(2,1)} %gather_project.1.kv_in) | copy-start | bytes 393220

commit v4 on v3

--- a/solution.py
+++ b/solution.py
@@ -9,7 +9,7 @@
 
 HEAD_DIM = 128
 RLEN = 128
-BATCH = 8
+SCORE_FACTOR = HEAD_DIM ** (-0.5) * math.log2(math.e)
 UNROLL = 4
 MESH = pl.DeviceIdType.MESH
 BF16 = jnp.bfloat16
@@ -36,13 +36,19 @@
     gain_hbm,
     kvbias_hbm,
     pos_hbm,
+    q_hbm,
+    tkv_hbm,
     out_ref,
+    text_sums,
+    text_max,
     mbias_ref,
     gain_ref,
     kvbias_ref,
     pos_ref,
     cos_ref,
     sin_ref,
+    q_in,
+    tkv_in,
     vis,
     act,
     wbuf,
@@ -156,6 +162,8 @@
                 (gain_hbm, gain_ref),
                 (kvbias_hbm, kvbias_ref),
                 (pos_hbm, pos_ref),
+                (tkv_hbm, tkv_in),
+                (q_hbm, q_in),
             )
         )
     ]
@@ -192,6 +200,13 @@
     own_w.wait()
     for half in (0, 1):
         w_send_to(0, half, dx=2)
+    send(
+        kvw_hbm.at[far_rows(lax.rem(z + 4, 8))],
+        far_piece(quarter),
+        kz_send.at[FAR_SLOT],
+        kz_recv.at[FAR_SLOT],
+        at(dz=4),
+    )
     for j in (1, 2, 3, 4, 5, 6):
         zz = lax.rem(z + ZOFF[j] + 8, 8)
         send(
@@ -201,13 +216,6 @@
             kz_recv.at[ZBACK[j]],
             at(dz=ZOFF[j]),
         )
-    send(
-        kvw_hbm.at[far_rows(lax.rem(z + 4, 8))],
-        far_piece(quarter),
-        kz_send.at[FAR_SLOT],
-        kz_recv.at[FAR_SLOT],
-        at(dz=4),
-    )
     for half in (0, 1):
         w_send_to(0, half, dy=1)
         w_send_to(0, 1 - half, dy=-1)
@@ -282,8 +290,37 @@
             block = kv_piece(first, count, rr * COLS + (1 - core) * ROWS, ROWS)
             arrived(block, kx_recv.at[group * 4 + i])
 
+    token = lax.rem(lax.broadcasted_iota(jnp.int32, (8 * RLEN, RLEN), 0), RLEN)
+    causal = lax.broadcasted_iota(jnp.int32, (8 * RLEN, RLEN), 1) <= token
+
+    def text(first, count):
+        def step(r, carry):
+            rows = pl.ds(pl.multiple_of(r * RLEN, RLEN), RLEN)
+            q = jnp.concatenate(
+                [q_in[rows, h * HEAD_DIM : (h + 1) * HEAD_DIM] for h in range(8)], axis=0
+            )
+            scores = lax.dot_general(
+                q,
+                tkv_in[rows, :HEAD_DIM],
+                (((1,), (1,)), ((), ())),
+                preferred_element_type=F32,
+            )
+            scores = jnp.where(causal, scores, -1e30)
+            highest = jnp.max(scores, axis=1, keepdims=True)
+            weights = jnp.exp2((scores - highest) * SCORE_FACTOR).astype(BF16)
+            values = jnp.concatenate(
+                [tkv_in[rows, HEAD_DIM:], jnp.ones((RLEN, HEAD_DIM), BF16)], axis=1
+            )
+            text_sums[r] = jnp.dot(weights, values, preferred_element_type=F32)
+            text_max[r] = jnp.broadcast_to(highest, (8 * RLEN, HEAD_DIM))
+            return carry
+
+        lax.fori_loop(first, first + count, step, 0)
+
     activate(0)
     activate(1)
+    for copy in small:
+        copy.wait()
     w_wait(NEXT_DOWN, 0)
     w_send_to(NEXT_DOWN, 0, dy=1)
     w_wait(NEXT_UP, 1)
@@ -303,6 +340,7 @@
     w_sibling(NEXT_UP)
     activate(5)
     kv_share(1)
+    far_share()
     w_wait(CROSS_DOWN, 0)
     w_send_to(CROSS_DOWN, 0, dy=1)
     w_wait(CROSS_UP, 1)
@@ -312,10 +350,7 @@
         w_wait(FAR, half)
     w_sibling(FAR)
     kv_share(2)
-    far_share()
     activate(7)
-    for copy in small:
-        copy.wait()
     mine = pl.ds(pl.multiple_of(roll * HALF, HALF), HALF)
     theirs = pl.ds(pl.multiple_of((1 - roll) * HALF, HALF), HALF)
     lane = lax.broadcasted_iota(jnp.int32, (HALF, HEAD_DIM), 1)
@@ -354,6 +389,7 @@
     partner = (g, 1 - roll, z)
     send(visual.at[theirs], xs.at[roll], v_sem.at[0], v_sem.at[1], partner)
     xs[roll] = visual[mine, :]
+    text(0, 2)
     for group in range(3):
         kv_end(group)
     far_end()
@@ -412,6 +448,7 @@
     sbuf[behind(1)] = product(behind(1)).astype(BF16)
     partial_send(behind(1), rbuf, ahead(1), -1)
     proj[...] = product(ahead(3))
+    text(2, 1)
     arrived(rbuf.at[7], p_recv.at[7])
     sbuf[ahead(3)] = (proj[...] + rbuf[7].astype(F32)).astype(BF16)
     partial_send(ahead(3), rbuf, behind(3), 3)
@@ -420,6 +457,7 @@
     sbuf[behind(2)] = (proj[...] + rbuf[0].astype(F32)).astype(BF16)
     partial_send(behind(2), rbuf, ahead(2), -2)
     proj[...] = product(0)
+    text(3, 3)
 
     def square_step(j, square):
         arrived(sumsq_in.at[j], q_recv.at[j])
@@ -438,6 +476,7 @@
     res[:, HEAD_DIM:] = value.astype(BF16)
     send(res, res_in, o_sem.at[0], o_sem.at[1], partner)
     out_ref[mine, :] = res[...]
+    text(6, 2)
     arrived(res_in, o_sem.at[1])
     out_ref[theirs, :] = res_in[...]
     for copy in started:
@@ -450,15 +489,21 @@
     lax.fori_loop(1, 8, sent_step, 0)
 
 
-def gather_project(vis, w, kvw, mbias, gain, kvbias, pos):
+def gather_project(vis, w, kvw, mbias, gain, kvbias, pos, q, tkv):
+    rollouts = q.shape[0] // RLEN
+    heads = q.shape[1] // HEAD_DIM
     vmem = pl.BlockSpec(memory_space=pltpu.VMEM)
     hbm = pl.BlockSpec(memory_space=pltpu.HBM)
     dma = pltpu.SemaphoreType.DMA
     return pl.pallas_call(
         gather_project_kernel,
-        out_shape=jax.ShapeDtypeStruct((ROWS, 2 * HEAD_DIM), BF16),
-        in_specs=[hbm] * 7,
-        out_specs=vmem,
+        out_shape=(
+            pltpu.VMEM((ROWS, 2 * HEAD_DIM), BF16),
+            pltpu.VMEM((rollouts, heads * RLEN, 2 * HEAD_DIM), F32),
+            pltpu.VMEM((rollouts, heads * RLEN, HEAD_DIM), F32),
+        ),
+        in_specs=[hbm] * 9,
+        out_specs=(vmem, vmem, vmem),
         scratch_shapes=[
             pltpu.VMEM((1, COLS), F32),
             pltpu.VMEM((1, 8192), F32),
@@ -466,6 +511,8 @@
             pltpu.VMEM((3, ROWS), jnp.int32),
             pltpu.VMEM((HALF, HEAD_DIM), F32),
             pltpu.VMEM((HALF, HEAD_DIM), F32),
+            pltpu.VMEM(q.shape, BF16),
+            pltpu.VMEM(tkv.shape, BF16),
             pltpu.VMEM((ROWS, 5120), BF16),
             pltpu.VMEM((8, ROWS, PAIR), BF16),
             pltpu.VMEM((8, PAIR, COLS), BF16),
@@ -481,7 +528,7 @@
             pltpu.VMEM((HALF, 2 * HEAD_DIM), F32),
             pltpu.VMEM((HALF, 2 * HEAD_DIM), BF16),
             pltpu.VMEM((HALF, 2 * HEAD_DIM), BF16),
-            dma((7,)),
+            dma((9,)),
             dma((32,)),
             dma((32,)),
             dma((8,)),
@@ -496,21 +543,22 @@
             dma((2,)),
         ],
         compiler_params=pltpu.CompilerParams(
-            collective_id=0, has_side_effects=True, vmem_limit_bytes=60 * 2**20
+            collective_id=0, has_side_effects=True, vmem_limit_bytes=46 * 2**20
         ),
         cost_estimate=pl.CostEstimate(
             flops=2_500_000_000, bytes_accessed=8_000_000, transcendentals=1_500_000
         ),
         name="gather_project",
-    )(vis, w, kvw, mbias, gain, kvbias, pos)
+    )(vis, w, kvw, mbias, gain, kvbias, pos, q, tkv)
 
 
 def attention_kernel(
     count_ref,
     length_ref,
     q_in,
-    tkv_in,
     kv_in,
+    text_sums,
+    text_max,
     out_hbm,
     out,
     keys,
@@ -520,84 +568,72 @@
     rollouts = length_ref.shape[0]
     live = lax.broadcasted_iota(jnp.int32, (ROWS, HEAD_DIM), 0) < count_ref[0]
     image_keys = kv_in[:, :HEAD_DIM]
-    image_keys = jnp.where(live, image_keys, image_keys[:1])
-    image_values = jnp.where(live, kv_in[:, HEAD_DIM:], 0.0).astype(BF16)
-    keys[...] = image_keys
-    values[:, :HEAD_DIM] = image_values
+    keys[...] = jnp.where(live, image_keys, image_keys[:1])
+    values[:, :HEAD_DIM] = jnp.where(live, kv_in[:, HEAD_DIM:], 0.0).astype(BF16)
     values[:, HEAD_DIM:] = jnp.where(live, 1.0, 0.0).astype(BF16)
-
-    batch = BATCH * RLEN
-    token = lax.rem(lax.broadcasted_iota(jnp.int32, (batch, RLEN), 0), RLEN)
-    causal = lax.broadcasted_iota(jnp.int32, (batch, RLEN), 1) <= token
-    factor = HEAD_DIM ** (-0.5) * math.log2(math.e)
+    token = lax.rem(lax.broadcasted_iota(jnp.int32, (8 * RLEN, RLEN), 0), RLEN)
+    heads = [slice(h * HEAD_DIM, (h + 1) * HEAD_DIM) for h in range(8)]
+
     def one(r):
         rows = pl.ds(pl.multiple_of(r * RLEN, RLEN), RLEN)
-        text_keys = tkv_in[rows, :HEAD_DIM]
-        text_values = jnp.concatenate(
-            [tkv_in[rows, HEAD_DIM:], jnp.ones((RLEN, HEAD_DIM), BF16)], axis=1
+        kept = token < length_ref[r]
+        q = jnp.concatenate([q_in[rows, cols] for cols in heads], axis=0)
+        scores = lax.dot_general(
+            q, keys[...], (((1,), (1,)), ((), ())), preferred_element_type=F32
         )
-        kept = token < length_ref[r]
-        for h in range(0, 8, BATCH):
-            heads = [slice(k * HEAD_DIM, (k + 1) * HEAD_DIM) for k in range(h, h + BATCH)]
-            q = jnp.concatenate([q_in[rows, cols] for cols in heads], axis=0)
-            image = lax.dot_general(
-                q, keys[...], (((1,), (1,)), ((), ())), preferred_element_type=F32
-            )
-            text = lax.dot_general(
-                q, text_keys, (((1,), (1,)), ((), ())), preferred_element_type=F32
-            )
-            text = jnp.where(causal, text, -1e30)
-            highest = jnp.maximum(
-                jnp.maximum(image[:, :HEAD_DIM], image[:, HEAD_DIM:]), text
-            )
-            highest = jnp.max(highest, axis=1, keepdims=True)
-            image = jnp.exp2((image - highest) * factor).astype(BF16)
-            text = jnp.exp2((text - highest) * factor).astype(BF16)
-            sums = jnp.dot(image, values[...], preferred_element_type=F32)
-            sums += jnp.dot(text, text_values, preferred_element_type=F32)
-            attended = jnp.where(kept, sums[:, :HEAD_DIM] / sums[:, HEAD_DIM:], 0.0).astype(BF16)
-            for i, cols in enumerate(heads):
-                out[r, :, cols] = attended[i * RLEN : (i + 1) * RLEN]
-
-    def rollout(step, carry):
-        for i in range(UNROLL):
-            one(step * UNROLL + i)
-        for i in range(UNROLL):
-            r = step * UNROLL + i
-            rows = pl.ds(pl.multiple_of(r * RLEN, RLEN), RLEN)
-            pltpu.make_async_copy(out.at[r], out_hbm.at[rows], out_sem.at[r]).start()
+        first, second = scores[:, :HEAD_DIM], scores[:, HEAD_DIM:]
+        text_highest = text_max[r]
+        highest = jnp.max(jnp.maximum(first, second), axis=1, keepdims=True)
+        highest = jnp.maximum(highest, text_highest)
+        first = jnp.exp2((first - highest) * SCORE_FACTOR)
+        second = jnp.exp2((second - highest) * SCORE_FACTOR)
+        scale = jnp.exp2((text_highest - highest) * SCORE_FACTOR)
+        weights = jnp.concatenate([first, second], axis=1).astype(BF16)
+        sums = jnp.dot(weights, values[...], preferred_element_type=F32)
+        top = sums[:, :HEAD_DIM] + text_sums[r, :, :HEAD_DIM] * scale
+        bottom = sums[:, HEAD_DIM:] + text_sums[r, :, HEAD_DIM:] * scale
+        attended = jnp.where(kept, top / bottom, 0.0).astype(BF16)
+        for i, cols in enumerate(heads):
+            out[r, :, cols] = attended[i * RLEN : (i + 1) * RLEN]
+
+    def store(r):
+        rows = pl.ds(pl.multiple_of(r * RLEN, RLEN), RLEN)
+        return pltpu.make_async_copy(out.at[r], out_hbm.at[rows], out_sem.at[r])
+
+    def step(i, carry):
+        for u in range(UNROLL):
+            one(i * UNROLL + u)
+        for u in range(UNROLL):
+            store(i * UNROLL + u).start()
         return carry
 
-    lax.fori_loop(0, rollouts // UNROLL, rollout, 0)
+    lax.fori_loop(0, rollouts // UNROLL, step, 0)
 
     def stored(r, carry):
-        rows = pl.ds(pl.multiple_of(r * RLEN, RLEN), RLEN)
-        pltpu.make_async_copy(out.at[r], out_hbm.at[rows], out_sem.at[r]).wait()
+        store(r).wait()
         return carry
 
     lax.fori_loop(0, rollouts, stored, 0)
 
 
-def attention(count, length, q, tkv, kv):
+def attention(count, length, q, kv, text_sums, text_max):
     rollouts = length.shape[0]
     smem = pl.BlockSpec(memory_space=pltpu.SMEM)
     vmem = pl.BlockSpec(memory_space=pltpu.VMEM)
-    hbm = pl.BlockSpec(memory_space=pl.ANY)
-    dma = pltpu.SemaphoreType.DMA
     return pl.pallas_call(
         attention_kernel,
-        in_specs=[smem, smem, vmem, vmem, vmem],
-        out_specs=hbm,
+        in_specs=[smem, smem, vmem, vmem, vmem, vmem],
+        out_specs=pl.BlockSpec(memory_space=pl.ANY),
         out_shape=jax.ShapeDtypeStruct(q.shape, BF16),
         scratch_shapes=[
             pltpu.VMEM((rollouts, RLEN, q.shape[1]), BF16),
             pltpu.VMEM((ROWS, HEAD_DIM), BF16),
             pltpu.VMEM((ROWS, 2 * HEAD_DIM), BF16),
-            dma((rollouts,)),
+            pltpu.SemaphoreType.DMA((rollouts,)),
         ],
-        compiler_params=pltpu.CompilerParams(vmem_limit_bytes=32 * 2**20),
+        compiler_params=pltpu.CompilerParams(vmem_limit_bytes=24 * 2**20),
         name="attention",
-    )(count, length, q, tkv, kv)
+    )(count, length, q, kv, text_sums, text_max)
 
 
 def body(
@@ -613,7 +649,7 @@
     image_pos,
     resp_length,
 ):
-    kv = gather_project(
+    kv, text_sums, text_max = gather_project(
         vis_hidden,
         merge_weight,
         kv_weight,
@@ -621,8 +657,10 @@
         norm_gain.reshape(1, -1),
         kv_bias.reshape(1, -1),
         image_pos,
+        queries,
+        text_kv,
     )
-    return attention(image_count, resp_length, queries, text_kv, kv)
+    return attention(image_count, resp_length, queries, kv, text_sums, text_max)
 
 
 def solution(mesh):

time: 66.5 us -> 62.5 us (0.940)
  Pallas kernels: 64.8 us -> 61.7 us
  local copies, waits for them, and re-layouts: 0.91 us -> 0.01 us
    pallas_call x2, Pallas kernels: 64.8 us -> 61.7 us  [the longest x1 56.5 us: gather_project(): pl.pallas_call(gather_project_kernel, out_shape=(pltpu.VMEM((ROWS, 2 * HE...]
    unnamed x8 -> x4, local copies, waits for them, and re-layouts: 0.91 us -> 0.01 us
where the time goes in v4:
time: 62.5 us; the launch traced here: 62.4 us
  Pallas kernels  61.7 us (99%)
  between operations  0.69 us (1%)
    pallas_call x1, Pallas kernels, gather_project(): pl.pallas_call(gather_project_kernel, out_shape=(pltpu.VMEM((ROWS, 2 * HE...  56.5 us
    pallas_call x1, Pallas kernels, attention(): pl.pallas_call(attention_kernel, in_specs=[smem, smem, vmem, vmem, vmem,...  5.25 us

profile of v4, /device:TPU:6, one launch (start us, length us, event | category | flops | bytes accessed | tf_op | source)
XLA Modules:
  0.0 62.4 jit_solution(18235828750737017800)
XLA Ops:
  0.7 0.0 copy-start
  0.7 0.0 copy-start.1
  0.7 56.5 %gather_project.1 = (bf16[256,256]{1,0:T(8,128)(2,1)S(1)}, f32[8,1024,256]{2,1,0:T(8,128)S(1)}, f32[8,1024,128]{2,1,0:T(8,128)S(1)}) custom-call(bf16[256,5120]{1,0:T(8,128)(2,1)} %vis_hbm.1, bf16[320,512]{1,0:T(8,128)(2,1)} %w_hbm.1, bf16[8192,256]{1,0:T(8,128)(2,1)} %kvw_hbm.1, f32[1,512]{1,0:T(1,128)} %bitcast.4, f32[1,8192]{1,0:T(1,128)} %bitcast.3, ...), custom_call_target="tpu_custom_call" | custom-call | flops 2500000000 | bytes 8000000 | tf_op jit(solution)/shard_map/gather_project/pallas_call | solution.py:498
  57.1 0.0 copy-done
  57.2 0.0 copy-done.1
  57.2 5.2 %attention.1 = bf16[1024,1024]{1,0:T(8,128)(2,1)} custom-call(s32[1]{0:T(128)S(6)} %copy.12.count_ref, s32[8]{0:T(128)S(1)} %copy-done.1, bf16[1024,1024]{1,0:T(8,128)(2,1)S(1)} %copy-done, bf16[256,256]{1,0:T(8,128)(2,1)S(1)} %get-tuple-element.8.kv_in, f32[8,1024,256]{2,1,0:T(8,128)S(1)} %get-tuple-element.9.text_sums, ...), custom_call_target="tpu_custom_call" | custom-call | tf_op jit(solution)/shard_map/attention/pallas_call | solution.py:623
Async XLA Ops:
  0.7 56.5 %copy-start = (bf16[1024,1024]{1,0:T(8,128)(2,1)S(1)}, bf16[1024,1024]{1,0:T(8,128)(2,1)}, u32[]{:S(2)}) copy-start(bf16[1024,1024]{1,0:T(8,128)(2,1)} %q_in.1) | copy-start | bytes 6291460
  0.7 56.5 %copy-start.1 = (s32[8]{0:T(128)S(1)}, s32[8]{0:T(128)}, u32[]{:S(2)}) copy-start(s32[8]{0:T(128)} %length_ref.1) | copy-start | bytes 100

commit v5 on v4

--- a/solution.py
+++ b/solution.py
@@ -10,7 +10,7 @@
 HEAD_DIM = 128
 RLEN = 128
 SCORE_FACTOR = HEAD_DIM ** (-0.5) * math.log2(math.e)
-UNROLL = 4
+UNROLL = 8
 MESH = pl.DeviceIdType.MESH
 BF16 = jnp.bfloat16
 F32 = jnp.float32
@@ -219,7 +219,6 @@
     for half in (0, 1):
         w_send_to(0, half, dy=1)
         w_send_to(0, 1 - half, dy=-1)
-    w_sibling(0)
 
     own_vis.wait()
 
@@ -333,6 +332,7 @@
         activate(3 + half)
     own_kv.wait()
     kv_share(0)
+    w_sibling(0)
     w_sibling(CROSS)
     w_wait(NEXT_DOWN, 1)
     w_sibling(NEXT_DOWN)
@@ -341,6 +341,7 @@
     activate(5)
     kv_share(1)
     far_share()
+    kv_pass(0)
     w_wait(CROSS_DOWN, 0)
     w_send_to(CROSS_DOWN, 0, dy=1)
     w_wait(CROSS_UP, 1)
@@ -364,7 +365,6 @@
     sin_ref[...] = jnp.where(lane < HEAD_DIM // 2, -sine, sine)
 
     acc[...] = jnp.broadcast_to(mbias_ref[...], acc.shape)
-    kv_pass(0)
     w_wait(CROSS_DOWN, 1)
     w_sibling(CROSS_DOWN)
     w_wait(CROSS_UP, 0)
@@ -372,15 +372,13 @@
     for slot in (0, NEXT_DOWN, NEXT_UP, FAR):
         w_sibling_wait(slot)
     merge(4, lambda i: hi * 4 + i)
-    kv_pass(1)
     for half in (0, 1):
         w_wait(CROSS_FAR, half)
         w_sibling(CROSS_FAR, half)
+    kv_pass(1)
     for slot in (CROSS, CROSS_DOWN, CROSS_UP):
         w_sibling_wait(slot)
     merge(3, lambda i: (1 - hi) * 4 + lax.rem(y + i + 3, 4))
-    kv_pass(2)
-    far_pass()
     for half in (0, 1):
         w_sibling_wait(CROSS_FAR, half)
     merge(1, lambda i: (1 - hi) * 4 + lax.rem(y + 2, 4))
@@ -388,6 +386,8 @@
     visual[...] = acc[...].astype(BF16)
     partner = (g, 1 - roll, z)
     send(visual.at[theirs], xs.at[roll], v_sem.at[0], v_sem.at[1], partner)
+    kv_pass(2)
+    far_pass()
     xs[roll] = visual[mine, :]
     text(0, 2)
     for group in range(3):
@@ -395,13 +395,11 @@
     far_end()
     arrived(xs.at[1 - roll], v_sem.at[1])
 
-    total = jnp.zeros((HALF, 1), F32)
+    def feature_start(r):
+        return pl.multiple_of(r * 4096 + z * COLS, COLS)
+
     for r in range(2):
-        start = pl.multiple_of(r * 4096 + z * COLS, COLS)
-        v = xs[r].astype(F32)
-        total += jnp.sum(v * v, axis=1, keepdims=True)
-        xg[r] = (v * gain_ref[:, pl.ds(start, COLS)]).astype(BF16)
-    sumsq[...] = jnp.broadcast_to(total, (HALF, HALF)).T[:8]
+        xg[r] = (xs[r].astype(F32) * gain_ref[:, pl.ds(feature_start(r), COLS)]).astype(BF16)
 
     def product(j):
         return jnp.dot(xg[0], kvbuf[j, :COLS], preferred_element_type=F32) + jnp.dot(
@@ -424,8 +422,6 @@
         sumsq_copy(i).start()
         return carry
 
-    lax.fori_loop(1, 8, sumsq_send, 0)
-
     way = 1 - 2 * core
 
     def ahead(k):
@@ -437,6 +433,13 @@
     def partial_send(j, dst, slot, steps):
         send(sbuf.at[j], dst.at[slot], p_send.at[j], p_recv.at[slot], at(dz=way * steps))
 
+    total = jnp.zeros((HALF, 1), F32)
+    for r in range(2):
+        v = xs[r].astype(F32)
+        total += jnp.sum(v * v, axis=1, keepdims=True)
+    sumsq[...] = jnp.broadcast_to(total, (HALF, HALF)).T[:8]
+    lax.fori_loop(1, 8, sumsq_send, 0)
+    proj[...] = product(ahead(3))
     sbuf[7] = product(7).astype(BF16)
     partial_send(7, rbuf, 7, 1)
     sbuf[behind(3)] = product(behind(3)).astype(BF16)
@@ -447,8 +450,6 @@
     partial_send(ahead(1), rbuf, behind(1), 1)
     sbuf[behind(1)] = product(behind(1)).astype(BF16)
     partial_send(behind(1), rbuf, ahead(1), -1)
-    proj[...] = product(ahead(3))
-    text(2, 1)
     arrived(rbuf.at[7], p_recv.at[7])
     sbuf[ahead(3)] = (proj[...] + rbuf[7].astype(F32)).astype(BF16)
     partial_send(ahead(3), rbuf, behind(3), 3)
@@ -457,7 +458,10 @@
     sbuf[behind(2)] = (proj[...] + rbuf[0].astype(F32)).astype(BF16)
     partial_send(behind(2), rbuf, ahead(2), -2)
     proj[...] = product(0)
-    text(3, 3)
+    text(2, 4)
+    for copy in started:
+        copy.wait_send()
+    started.clear()
 
     def square_step(j, square):
         arrived(sumsq_in.at[j], q_recv.at[j])
@@ -603,7 +607,6 @@
     def step(i, carry):
         for u in range(UNROLL):
             one(i * UNROLL + u)
-        for u in range(UNROLL):
             store(i * UNROLL + u).start()
         return carry
 

time: 62.5 us -> 61.3 us (0.981)
  Pallas kernels: 61.7 us -> 60.5 us
    pallas_call x1, Pallas kernels: 56.5 us -> 55.8 us  [gather_project(): pl.pallas_call(gather_project_kernel, out_shape=(pltpu.VMEM((ROWS, 2 * HE...]
where the time goes in v5:
time: 61.3 us; the launch traced here: 61.2 us
  Pallas kernels  60.5 us (99%)
  between operations  0.69 us (1%)
    pallas_call x1, Pallas kernels, gather_project(): pl.pallas_call(gather_project_kernel, out_shape=(pltpu.VMEM((ROWS, 2 * HE...  55.8 us
    pallas_call x1, Pallas kernels, attention(): pl.pallas_call(attention_kernel, in_specs=[smem, smem, vmem, vmem, vmem,...  4.67 us

profile of v5, /device:TPU:6, one launch (start us, length us, event | category | flops | bytes accessed | tf_op | source)
XLA Modules:
  0.0 61.2 jit_solution(10095750551413652965)
XLA Ops:
  0.7 0.0 copy-start
  0.7 0.0 copy-start.1
  0.7 55.8 %gather_project.1 = (bf16[256,256]{1,0:T(8,128)(2,1)S(1)}, f32[8,1024,256]{2,1,0:T(8,128)S(1)}, f32[8,1024,128]{2,1,0:T(8,128)S(1)}) custom-call(bf16[256,5120]{1,0:T(8,128)(2,1)} %vis_hbm.1, bf16[320,512]{1,0:T(8,128)(2,1)} %w_hbm.1, bf16[8192,256]{1,0:T(8,128)(2,1)} %kvw_hbm.1, f32[1,512]{1,0:T(1,128)} %bitcast.4, f32[1,8192]{1,0:T(1,128)} %bitcast.3, ...), custom_call_target="tpu_custom_call" | custom-call | flops 2500000000 | bytes 8000000 | tf_op jit(solution)/shard_map/gather_project/pallas_call | solution.py:502
  56.5 0.0 copy-done
  56.5 0.0 copy-done.1
  56.5 4.7 %attention.1 = bf16[1024,1024]{1,0:T(8,128)(2,1)} custom-call(s32[1]{0:T(128)S(6)} %copy.12.count_ref, s32[8]{0:T(128)S(1)} %copy-done.1, bf16[1024,1024]{1,0:T(8,128)(2,1)S(1)} %copy-done, bf16[256,256]{1,0:T(8,128)(2,1)S(1)} %get-tuple-element.8.kv_in, f32[8,1024,256]{2,1,0:T(8,128)S(1)} %get-tuple-element.9.text_sums, ...), custom_call_target="tpu_custom_call" | custom-call | tf_op jit(solution)/shard_map/attention/pallas_call | solution.py:626
Async XLA Ops:
  0.7 55.8 %copy-start = (bf16[1024,1024]{1,0:T(8,128)(2,1)S(1)}, bf16[1024,1024]{1,0:T(8,128)(2,1)}, u32[]{:S(2)}) copy-start(bf16[1024,1024]{1,0:T(8,128)(2,1)} %q_in.1) | copy-start | bytes 6291460
  0.7 55.8 %copy-start.1 = (s32[8]{0:T(128)S(1)}, s32[8]{0:T(128)}, u32[]{:S(2)}) copy-start(s32[8]{0:T(128)} %length_ref.1) | copy-start | bytes 100

commit v6 on v5

--- a/solution.py
+++ b/solution.py
@@ -62,6 +62,7 @@
     sbuf,
     rbuf,
     proj,
+    own_part,
     res,
     res_in,
     local_sem,
@@ -393,13 +394,19 @@
     for group in range(3):
         kv_end(group)
     far_end()
+    def weigh(r):
+        start = pl.multiple_of(r * 4096 + z * COLS, COLS)
+        xg[r] = (xs[r].astype(F32) * gain_ref[:, pl.ds(start, COLS)]).astype(BF16)
+
+    def half_product(j, r):
+        rows = pl.ds(pl.multiple_of(r * COLS, COLS), COLS)
+        return jnp.dot(xg[r], kvbuf[j, rows], preferred_element_type=F32)
+
+    weigh(roll)
+    own_part[0] = half_product(7, roll)
+    own_part[1] = half_product(6 - core, roll)
     arrived(xs.at[1 - roll], v_sem.at[1])
-
-    def feature_start(r):
-        return pl.multiple_of(r * 4096 + z * COLS, COLS)
-
-    for r in range(2):
-        xg[r] = (xs[r].astype(F32) * gain_ref[:, pl.ds(feature_start(r), COLS)]).astype(BF16)
+    weigh(1 - roll)
 
     def product(j):
         return jnp.dot(xg[0], kvbuf[j, :COLS], preferred_element_type=F32) + jnp.dot(
@@ -440,9 +447,9 @@
     sumsq[...] = jnp.broadcast_to(total, (HALF, HALF)).T[:8]
     lax.fori_loop(1, 8, sumsq_send, 0)
     proj[...] = product(ahead(3))
-    sbuf[7] = product(7).astype(BF16)
+    sbuf[7] = (own_part[0] + half_product(7, 1 - roll)).astype(BF16)
     partial_send(7, rbuf, 7, 1)
-    sbuf[behind(3)] = product(behind(3)).astype(BF16)
+    sbuf[behind(3)] = (own_part[1] + half_product(behind(3), 1 - roll)).astype(BF16)
     partial_send(behind(3), rbuf, 0, -1)
     sbuf[ahead(2)] = product(ahead(2)).astype(BF16)
     partial_send(ahead(2), rbuf, behind(2), 2)
@@ -530,6 +537,7 @@
             pltpu.VMEM((8, HALF, 2 * HEAD_DIM), BF16),
             pltpu.VMEM((8, HALF, 2 * HEAD_DIM), BF16),
             pltpu.VMEM((HALF, 2 * HEAD_DIM), F32),
+            pltpu.VMEM((2, HALF, 2 * HEAD_DIM), F32),
             pltpu.VMEM((HALF, 2 * HEAD_DIM), BF16),
             pltpu.VMEM((HALF, 2 * HEAD_DIM), BF16),
             dma((9,)),

time: 61.3 us -> 61.2 us (level)
  no operation moved by 1% of the time
where the time goes in v6:
time: 61.2 us; the launch traced here: 61.1 us
  Pallas kernels  60.4 us (99%)
  between operations  0.69 us (1%)
    pallas_call x1, Pallas kernels, gather_project(): pl.pallas_call(gather_project_kernel, out_shape=(pltpu.VMEM((ROWS, 2 * HE...  55.8 us
    pallas_call x1, Pallas kernels, attention(): pl.pallas_call(attention_kernel, in_specs=[smem, smem, vmem, vmem, vmem,...  4.67 us

profile of v6, /device:TPU:6, one launch (start us, length us, event | category | flops | bytes accessed | tf_op | source)
XLA Modules:
  0.0 61.1 jit_solution(1951995975716770966)
XLA Ops:
  0.7 0.0 copy-start
  0.7 0.0 copy-start.1
  0.7 55.8 %gather_project.1 = (bf16[256,256]{1,0:T(8,128)(2,1)S(1)}, f32[8,1024,256]{2,1,0:T(8,128)S(1)}, f32[8,1024,128]{2,1,0:T(8,128)S(1)}) custom-call(bf16[256,5120]{1,0:T(8,128)(2,1)} %vis_hbm.1, bf16[320,512]{1,0:T(8,128)(2,1)} %w_hbm.1, bf16[8192,256]{1,0:T(8,128)(2,1)} %kvw_hbm.1, f32[1,512]{1,0:T(1,128)} %bitcast.4, f32[1,8192]{1,0:T(1,128)} %bitcast.3, ...), custom_call_target="tpu_custom_call" | custom-call | flops 2500000000 | bytes 8000000 | tf_op jit(solution)/shard_map/gather_project/pallas_call | solution.py:509
  56.5 0.0 copy-done
  56.5 0.0 copy-done.1
  56.5 4.7 %attention.1 = bf16[1024,1024]{1,0:T(8,128)(2,1)} custom-call(s32[1]{0:T(128)S(6)} %copy.12.count_ref, s32[8]{0:T(128)S(1)} %copy-done.1, bf16[1024,1024]{1,0:T(8,128)(2,1)S(1)} %copy-done, bf16[256,256]{1,0:T(8,128)(2,1)S(1)} %get-tuple-element.8.kv_in, f32[8,1024,256]{2,1,0:T(8,128)S(1)} %get-tuple-element.9.text_sums, ...), custom_call_target="tpu_custom_call" | custom-call | tf_op jit(solution)/shard_map/attention/pallas_call | solution.py:634
Async XLA Ops:
  0.7 55.8 %copy-start = (bf16[1024,1024]{1,0:T(8,128)(2,1)S(1)}, bf16[1024,1024]{1,0:T(8,128)(2,1)}, u32[]{:S(2)}) copy-start(bf16[1024,1024]{1,0:T(8,128)(2,1)} %q_in.1) | copy-start | bytes 6291460
  0.7 55.8 %copy-start.1 = (s32[8]{0:T(128)S(1)}, s32[8]{0:T(128)}, u32[]{:S(2)}) copy-start(s32[8]{0:T(128)} %length_ref.1) | copy-start | bytes 100
